TPU v7x, 32 devices: a whole 2x2x4 slice. The times are simulated.
32 devices in a mesh: seq: 32 (over z, y, x, core), head: 1.
Axes of the slice: x: 2, y: 2, z: 4, core: 2. Of those that a mesh axis runs over, the one named last changes fastest.
Arguments:
- queries: bfloat16 [2048, 1536], P('seq', 'head'), may hold values from -6 to 6
- key_vectors: bfloat16 [2048, 512], P('seq', 'head'), may hold values from -6 to 6
- value_vectors: bfloat16 [2048, 512], P('seq', 'head'), may hold values from -6 to 6
- lengths: int32 [16], replicated, may hold values from 1 to 256, 2048 in all
- out_weight: bfloat16 [1536, 1536], P('head', 'seq'), may hold values from -0.15625 to 0.15625
- residual: bfloat16 [2048, 1536], P(('seq', 'head')), may hold values from -6 to 6
- norm_gain: float32 [1536], replicated, may hold values from 0.1 to 1.9
- route_ids: int32 [2048, 6], P(('seq', 'head')), may hold values from 0 to 63, all different within a row; in each aligned block of 64 rows (0 to 63, 64 to 127, ...) at most 6 rows name the same one
- route_logits: float32 [2048, 6], P(('seq', 'head')), may hold values from -8 to 340
- shared_gate_up: bfloat16 [1536, 2, 1024], P(None, None, ('seq', 'head')), may hold values from -0.15625 to 0.15625
- shared_down: bfloat16 [1024, 1536], P(('seq', 'head')), may hold values from -0.1875 to 0.1875
- expert_gate_up: bfloat16 [128, 1536, 2, 256], P('seq'), may hold values from -0.15625 to 0.15625
- expert_down: bfloat16 [128, 256, 1536], P('seq'), may hold values from -0.25 to 0.25
- cache_blocks: bfloat16 [32, 128, 8, 4, 128], P('seq', None, None, 'head'), may hold values from -6 to 6
- block_table: int32 [32], replicated, may hold values from 0 to 31, each once
Outputs:
- layer_out: bfloat16 [2048, 1536], P(('seq', 'head'))
- cache_out: bfloat16 [32, 128, 8, 4, 128], P(None, 'seq', None, 'head')
Inputs may be any that keep to these rules, and one draw needn't show every extreme that they name: The lengths sum to 2048. `route_ids`: each token names 6 different experts; among the tokens of one device no expert is named more than 6 times. `block_table`: every block appears once.
All inputs are finite; a program needn't handle non-finite values.
Results may differ from a plain program's by a relative error of at most 0.0095.
Values may be sent and summed in bfloat16 or wider, within the bound.
No kernel may reach another device: no remote copies, remote signals or barrier semaphores. Data moves between devices by JAX's collectives and lax.ppermute only.
A program may use at most 64 MiB of HBM per device.

v0:
```python
import math

import jax
import jax.numpy as jnp
from jax import lax
from jax.sharding import PartitionSpec as P

HD = 128
EXPERTS = 64
TOP = 6
REACH = 4
HALVES = 128
CAP = 6


NEGATIVE = -1e30
EPSILON = 1e-05


def from_behind(shard, axis, by):
    devices = lax.axis_size(axis)
    pairs = [(i, i + by) for i in range(devices) if 0 <= i + by < devices]
    return lax.ppermute(shard, axis, pairs)


def segment_of(positions, lengths):
    request_ends = jnp.cumsum(lengths)
    passed = (request_ends[None, :] <= positions[:, None]).astype(jnp.int32)
    return jnp.sum(passed, axis=1)


def shared_ffn(rows_in, gate_up_part, down_part):
    shared_both = jnp.einsum(
        "td,dcf->tcf", rows_in, gate_up_part, preferred_element_type=jnp.float32
    )
    shared_act = (jax.nn.silu(shared_both[:, 0]) * shared_both[:, 1]).astype(jnp.bfloat16)
    return jnp.dot(shared_act, down_part, preferred_element_type=jnp.float32)


def shards(
    queries,
    key_vectors,
    value_vectors,
    lengths,
    out_weight,
    residual,
    norm_gain,
    route_ids,
    route_logits,
    shared_gate_up,
    shared_down,
    expert_gate_up,
    expert_down,
    cache_blocks,
    block_table,
):
    handed = lax.all_to_all(cache_blocks, "seq", split_axis=1, concat_axis=0, tiled=True)
    cache_out = jnp.take(handed, block_table, axis=0)
    tok_rows = queries.shape[0]
    seq_index = lax.axis_index("seq")
    earlier = [
        from_behind((key_vectors, value_vectors), "seq", offset) for offset in range(REACH, 0, -1)
    ]
    window_keys = jnp.concatenate([member[0] for member in earlier] + [key_vectors], axis=0)
    window_values = jnp.concatenate([member[1] for member in earlier] + [value_vectors], axis=0)
    key_count = window_keys.shape[0]
    kv_heads = key_vectors.shape[1] // HD
    query_heads = queries.shape[1] // HD
    group_size = query_heads // kv_heads
    query_pos = seq_index * tok_rows + jnp.arange(tok_rows, dtype=jnp.int32)
    key_pos = (seq_index - REACH) * tok_rows + jnp.arange(key_count, dtype=jnp.int32)
    visible = (key_pos[None, :] >= 0) & (key_pos[None, :] <= query_pos[:, None])
    visible = visible & (
        segment_of(key_pos, lengths)[None, :] == segment_of(query_pos, lengths)[:, None]
    )
    query_part = queries.reshape(tok_rows, kv_heads, group_size, HD)
    key_part = window_keys.reshape(key_count, kv_heads, HD)
    value_part = window_values.reshape(key_count, kv_heads, HD)
    scores = jnp.einsum(
        "tkgd,wkd->kgtw", query_part, key_part, preferred_element_type=jnp.float32
    ) * (1.0 / math.sqrt(HD))
    scores = jnp.where(visible[None, None], scores, NEGATIVE)
    row_max = jnp.max(scores, axis=-1, keepdims=True)
    weights = jnp.exp(scores - row_max)
    row_total = jnp.sum(weights, axis=-1)
    weighted = jnp.einsum(
        "kgtw,wkd->tkgd",
        weights.astype(jnp.bfloat16),
        value_part,
        preferred_element_type=jnp.float32,
    )
    heads = (weighted / jnp.transpose(row_total, (2, 0, 1))[..., None]).astype(jnp.bfloat16)
    heads = heads.reshape(tok_rows, query_heads * HD)
    partial_out = jnp.dot(
        heads,
        lax.all_gather(out_weight, "seq", axis=1, tiled=True),
        preferred_element_type=jnp.float32,
    )
    attn_out = lax.psum_scatter(partial_out, "head", scatter_dimension=0, tiled=True)
    mixed = residual.astype(jnp.float32) + attn_out
    mean_square = jnp.mean(mixed * mixed, axis=-1, keepdims=True)
    normed = (mixed * lax.rsqrt(mean_square + EPSILON) * norm_gain).astype(jnp.bfloat16)
    gate_up_all, down_all = (
        lax.all_gather(shared_gate_up, ("seq", "head"), axis=2, tiled=True),
        lax.all_gather(shared_down, ("seq", "head"), axis=0, tiled=True),
    )
    shared_part = shared_ffn(normed, gate_up_all, down_all)
    own_tokens = normed.shape[0]
    width_model = normed.shape[1]
    flat_ids = route_ids.reshape(-1)
    onehot = (flat_ids[:, None] == jnp.arange(EXPERTS, dtype=jnp.int32)[None, :]).astype(jnp.int32)
    slot_rank = jnp.sum((jnp.cumsum(onehot, axis=0) - 1) * onehot, axis=1)
    first_slot = flat_ids * CAP + slot_rank
    second_slot = (flat_ids + EXPERTS) * CAP + slot_rank
    token_of = jnp.arange(flat_ids.shape[0], dtype=jnp.int32) // TOP
    routed_rows = normed[token_of]
    outgoing = jnp.zeros((HALVES * CAP, width_model), jnp.bfloat16)
    outgoing = outgoing.at[jnp.concatenate([first_slot, second_slot])].set(
        jnp.concatenate([routed_rows, routed_rows], axis=0)
    )
    local_halves = expert_gate_up.shape[0]
    outgoing = outgoing.reshape(HALVES // local_halves, local_halves, CAP, width_model)
    gate_up = jnp.einsum(
        "nsjd,sdcf->nsjcf",
        lax.all_to_all(outgoing, "seq", split_axis=0, concat_axis=0, tiled=True),
        expert_gate_up,
        preferred_element_type=jnp.float32,
    )
    expert_act = (jax.nn.silu(gate_up[:, :, :, 0]) * gate_up[:, :, :, 1]).astype(jnp.bfloat16)
    half_out = jnp.einsum(
        "nsjf,sfd->nsjd", expert_act, expert_down, preferred_element_type=jnp.float32
    ).astype(jnp.bfloat16)
    returned = lax.all_to_all(half_out, "seq", split_axis=0, concat_axis=0, tiled=True)
    returned = returned.reshape(HALVES * CAP, width_model)
    pair_sum = returned[first_slot].astype(jnp.float32) + returned[second_slot].astype(jnp.float32)
    route_probs = jax.nn.softmax(route_logits, axis=-1)
    routed = jnp.sum(
        route_probs[:, :, None] * pair_sum.reshape(own_tokens, TOP, width_model), axis=1
    )
    layer_out = (mixed + shared_part + routed).astype(jnp.bfloat16)
    return (layer_out, cache_out)


def solution(mesh):
    in_specs = (
        P("seq", "head"),
        P("seq", "head"),
        P("seq", "head"),
        P(),
        P("head", "seq"),
        P(("seq", "head"), None),
        P(),
        P(("seq", "head"), None),
        P(("seq", "head"), None),
        P(None, None, ("seq", "head")),
        P(("seq", "head"), None),
        P("seq", None, None, None),
        P("seq", None, None),
        P("seq", None, None, "head", None),
        P(),
    )
    out_specs = (P(("seq", "head"), None), P(None, "seq", None, "head", None))
    return jax.shard_map(shards, mesh=mesh, in_specs=in_specs, out_specs=out_specs, check_vma=False)
```

profile of v0, /device:TPU:10, one launch (start us, length us, event | category | flops | bytes accessed | tf_op | source)
XLA Modules:
  0.0 312.5 jit_solution(11663371336472502224)
XLA Ops:
  8.7 3.4 %collective-permute-start.4 = (bf16[64,512]{1,0:T(8,128)(2,1)}, bf16[64,512]{1,0:T(8,128)(2,1)S(1)}, u32[]{:S(2)}, u32[]{:S(2)}) collective-permute-start(bf16[64,512]{1,0:T(8,128)(2,1)} %param.16), channel_id=1, source_target_pairs={{0,4},{1,5},{2,6},{3,7},{4,8},{5,9},{6,10},{7,11},{8,12},{9,13},{1... | collective-permute-start | bytes 196616 | tf_op jit(solution)/shard_map/ppermute | solution.py:23
  14.7 3.4 %collective-permute-start.6 = (bf16[64,512]{1,0:T(8,128)(2,1)}, bf16[64,512]{1,0:T(8,128)(2,1)}, u32[]{:S(2)}, u32[]{:S(2)}) collective-permute-start(bf16[64,512]{1,0:T(8,128)(2,1)} %param.16), channel_id=1, source_target_pairs={{0,2},{1,3},{2,4},{3,5},{4,6},{5,7},{6,8},{7,9},{8,10},{9,11},{10,... | collective-permute-start | bytes 196616 | tf_op jit(solution)/shard_map/ppermute | solution.py:23
  20.7 3.4 %collective-permute-start = (bf16[64,512]{1,0:T(8,128)(2,1)}, bf16[64,512]{1,0:T(8,128)(2,1)}, u32[]{:S(2)}, u32[]{:S(2)}) collective-permute-start(bf16[64,512]{1,0:T(8,128)(2,1)} %param.17), channel_id=1, source_target_pairs={{0,4},{1,5},{2,6},{3,7},{4,8},{5,9},{6,10},{7,11},{8,12},{9,13},{1... | collective-permute-start | bytes 196616 | tf_op jit(solution)/shard_map/ppermute | solution.py:23
  30.8 3.6 %collective-permute-start.1 = (bf16[64,512]{1,0:T(8,128)(2,1)}, bf16[64,512]{1,0:T(8,128)(2,1)}, u32[]{:S(2)}, u32[]{:S(2)}) collective-permute-start(bf16[64,512]{1,0:T(8,128)(2,1)} %param.17), channel_id=1, source_target_pairs={{0,3},{1,4},{2,5},{3,6},{4,7},{5,8},{6,9},{7,10},{8,11},{9,12},{10... | collective-permute-start | bytes 196616 | tf_op jit(solution)/shard_map/ppermute | solution.py:23
  35.3 3.4 %collective-permute-start.2 = (bf16[64,512]{1,0:T(8,128)(2,1)}, bf16[64,512]{1,0:T(8,128)(2,1)}, u32[]{:S(2)}, u32[]{:S(2)}) collective-permute-start(bf16[64,512]{1,0:T(8,128)(2,1)} %param.17), channel_id=1, source_target_pairs={{0,2},{1,3},{2,4},{3,5},{4,6},{5,7},{6,8},{7,9},{8,10},{9,11},{10,... | collective-permute-start | bytes 196616 | tf_op jit(solution)/shard_map/ppermute | solution.py:23
  52.4 24.2 %all-gather.4.cloned.1.call-done = bf16[1536,1536]{0,1:T(8,128)(2,1)} async-done(((bf16[1536,48]{0,1:T(8,128)(2,1)}), bf16[1536,1536]{0,1:T(8,128)(2,1)}) %all-gather.4.cloned.1.call-update) | async-done | bytes 4718608 | tf_op jit(solution)/shard_map/all_gather | solution.py:96
  76.6 4.0 %multiply_reduce_fusion.1 = (f32[64]{0:T(128)S(1)}, f32[64,1536]{1,0:T(8,128)S(1)}) fusion(bf16[64,1536]{1,0:T(8,128)(2,1)} %reshape.368, bf16[1536,1536]{0,1:T(8,128)(2,1)} %all-gather.4.cloned.1.call-done, bf16[64,1536]{1,0:T(8,128)(2,1)} %param.20), kind=kOutput, calls=%fused_computation.40 | convolution fusion | flops 302383040 | bytes 5505280 | tf_op jit(solution)/shard_map/dot_general | solution.py:94
  81.5 2.8 gather_fusion
  84.4 9.1 %scatter_custom_fusion = bf16[768,1536]{1,0:T(8,128)(2,1)} fusion(s32[768]{0:T(1024)S(1)} %fusion.45, bf16[384,1536]{1,0:T(8,128)(2,1)} %gather_fusion, bf16[]{:T(256)} %constant.85, bf16[]{:T(256)} %constant.44.clone.1), kind=kCustom, calls=%fused_computation.11 | custom fusion | flops 4718592 | bytes 3538948 | tf_op jit(solution)/shard_map/scatter | solution.py:118
  93.4 5.0 %reshape.371 = bf16[32,4,6,1536]{3,2,1,0:T(8,128)(2,1)} reshape(bf16[768,1536]{1,0:T(8,128)(2,1)} %scatter_custom_fusion) | data formatting | bytes 4718592 | tf_op jit(solution)/shard_map/reshape | solution.py:122
  98.4 3.1 copy.86
  101.5 80.8 %all_to_all.22 = bf16[32,4,6,1536]{3,1,2,0:T(4,128)(2,1)} all-to-all(bf16[32,4,6,1536]{3,1,2,0:T(4,128)(2,1)S(1)} %copy.86), channel_id=1, replica_groups=mesh['seq'=32,'head'=1] {'seq'}, dimensions={0} | all-to-all | bytes 4718592 | tf_op jit(solution)/shard_map/all_to_all | solution.py:125
  182.3 5.0 %all-to-all-start.2 = ((bf16[1,128,8,4,128]{4,3,2,0,1:T(4,128)(2,1)}), bf16[1,128,8,4,128]{4,3,2,0,1:T(4,128)(2,1)}, u32[]{:S(2)}, u32[]{:S(2)}) async-start(bf16[1,128,8,4,128]{4,3,2,0,1:T(4,128)(2,1)} %bitcast.80), calls=%async_computation.2 | async-start | bytes 2097152 | tf_op jit(solution)/shard_map/all_to_all | solution.py:57
  188.0 5.2 %fusion.13 = f32[32,4,6,2,256]{4,0,3,2,1:T(8,128)S(1)} fusion(bf16[4,1536,2,256,1]{3,2,1,0,4:T(2,128)(2,1)} %bitcast.86, bf16[32,4,6,1536,1]{3,1,2,0,4:T(4,128)(2,1)} %bitcast.79), kind=kOutput, calls=%fused_computation.21 | convolution fusion | flops 1207959552 | bytes 10223616 | tf_op jit(solution)/shard_map/nsjd,sdcf->nsjcf/dot_general | solution.py:123
  194.1 3.2 %copy.90 = bf16[32,4,6,1536]{3,1,2,0:T(4,128)(2,1)} copy(bf16[32,4,6,1536]{3,0,2,1:T(8,128)(2,1)S(1)} %fusion.3) | data formatting | bytes 4718592 | tf_op jit(solution)/shard_map/convert_element_type | solution.py:132
  197.3 17.0 %all-to-all-done.2 = bf16[1,128,8,4,128]{4,3,2,0,1:T(4,128)(2,1)} async-done(((bf16[1,128,8,4,128]{4,3,2,0,1:T(4,128)(2,1)}), bf16[1,128,8,4,128]{4,3,2,0,1:T(4,128)(2,1)}, u32[]{:S(2)}, u32[]{:S(2)}) %all-to-all-start.2) | async-done | bytes 1048608 | tf_op jit(solution)/shard_map/all_to_all | solution.py:57
  214.3 5.0 %all-to-all-start.1 = ((bf16[32,4,6,1536]{3,1,2,0:T(4,128)(2,1)}), bf16[32,4,6,1536]{3,1,2,0:T(4,128)(2,1)S(1)}, u32[]{:S(2)}, u32[]{:S(2)}) async-start(bf16[32,4,6,1536]{3,1,2,0:T(4,128)(2,1)} %copy.90), calls=%async_computation.1 | async-start | bytes 4718592 | tf_op jit(solution)/shard_map/all_to_all | solution.py:133
  223.0 2.9 gather_fusion.3
  228.8 5.6 %fusion.35 = f32[64,2,1024]{2,0,1:T(8,128)} fusion(bf16[1536,2,1024]{0,2,1:T(8,128)(2,1)} %all-gather.6.cloned.1.call-done, bf16[64,1536]{1,0:T(8,128)(2,1)S(1)} %multiply_convert_fusion), kind=kOutput, calls=%fused_computation.47 | convolution fusion | flops 402653184 | bytes 7012352 | tf_op jit(solution)/shard_map/td,dcf->tcf/dot_general | solution.py:33
  234.4 48.6 %all-to-all-done.1 = bf16[32,4,6,1536]{3,1,2,0:T(4,128)(2,1)S(1)} async-done(((bf16[32,4,6,1536]{3,1,2,0:T(4,128)(2,1)}), bf16[32,4,6,1536]{3,1,2,0:T(4,128)(2,1)S(1)}, u32[]{:S(2)}, u32[]{:S(2)}) %all-to-all-start.1) | async-done | bytes 2359328 | tf_op jit(solution)/shard_map/all_to_all | solution.py:133
  285.4 3.7 %reshape.372 = bf16[768,1536]{1,0:T(8,128)(2,1)S(1)} reshape(bf16[32,4,6,1536]{3,2,1,0:T(8,128)(2,1)} %copy.91) | data formatting | bytes 4718592 | tf_op jit(solution)/shard_map/reshape | solution.py:134
  289.1 2.8 gather_fusion.1
  298.6 4.0 %multiply_reduce_fusion = f32[64,1536]{1,0:T(8,128)} fusion(f32[64,6,1536]{2,1,0:T(8,128)} %add.221, f32[64,6]{1,0:T(8,128)} %copy.82), kind=kLoop, calls=%fused_computation.9 | loop fusion | flops 1081344 | bytes 2754048 | tf_op jit(solution)/shard_map/reduce_sum | solution.py:137
  302.5 3.4 %fusion.12 = bf16[64,1536]{1,0:T(8,128)(2,1)} fusion(f32[64,1536]{1,0:T(8,128)} %multiply_reduce_fusion, f32[64,1536]{1,0:T(8,128)S(1)} %copy-done.3, bf16[1024,1536]{1,0:T(8,128)(2,1)} %all-gather.8.cloned.1.call-done, f32[64,2,1024]{2,0,1:T(8,128)} %fusion.35), kind=kOutput, calls=%fused_computation.20 | convolution fusion | flops 202014720 | bytes 4653056 | tf_op jit(solution)/shard_map/dot_general | solution.py:37
  (106 shorter events, 45.8 us)
Async XLA Ops:
  7.2 186.1 %copy-start = (bf16[4,256,1536]{2,1,0:T(8,128)(2,1)S(1)}, bf16[4,256,1536]{2,1,0:T(8,128)(2,1)}, u32[]{:S(2)}) copy-start(bf16[4,256,1536]{2,1,0:T(8,128)(2,1)} %param.27) | copy-start | bytes 9437188
  7.2 41.0 %copy-start.5 = (bf16[64,512]{1,0:T(8,128)(2,1)S(1)}, bf16[64,512]{1,0:T(8,128)(2,1)}, u32[]{:S(2)}) copy-start(bf16[64,512]{1,0:T(8,128)(2,1)} %param.17) | copy-start | bytes 196612
  7.2 69.4 %all-gather.4.cloned.1.call-start = ((), (), s32[]{:S(2)}) async-start(), calls=%async_computation.3 | async-start | bytes 4866048 | tf_op jit(solution)/shard_map/all_gather | solution.py:96
  7.9 220.9 %all-gather.6.cloned.1.call-start = ((), (), s32[]{:S(2)}) async-start(), calls=%async_computation.4 | async-start | bytes 6488064 | tf_op jit(solution)/shard_map/all_gather | solution.py:104
  8.7 21.5 %collective-permute-start.4 = (bf16[64,512]{1,0:T(8,128)(2,1)}, bf16[64,512]{1,0:T(8,128)(2,1)S(1)}, u32[]{:S(2)}, u32[]{:S(2)}) collective-permute-start(bf16[64,512]{1,0:T(8,128)(2,1)} %param.16), channel_id=1, source_target_pairs={{0,4},{1,5},{2,6},{3,7},{4,8},{5,9},{6,10},{7,11},{8,12},{9,13},{1... | collective-permute-start | bytes 196616 | tf_op jit(solution)/shard_map/ppermute | solution.py:23
  12.1 23.2 %collective-permute-start.5 = (bf16[64,512]{1,0:T(8,128)(2,1)}, bf16[64,512]{1,0:T(8,128)(2,1)}, u32[]{:S(2)}, u32[]{:S(2)}) collective-permute-start(bf16[64,512]{1,0:T(8,128)(2,1)} %param.16), channel_id=1, source_target_pairs={{0,3},{1,4},{2,5},{3,6},{4,7},{5,8},{6,9},{7,10},{8,11},{9,12},{10... | collective-permute-start | bytes 196616 | tf_op jit(solution)/shard_map/ppermute | solution.py:23
  14.7 24.9 %collective-permute-start.6 = (bf16[64,512]{1,0:T(8,128)(2,1)}, bf16[64,512]{1,0:T(8,128)(2,1)}, u32[]{:S(2)}, u32[]{:S(2)}) collective-permute-start(bf16[64,512]{1,0:T(8,128)(2,1)} %param.16), channel_id=1, source_target_pairs={{0,2},{1,3},{2,4},{3,5},{4,6},{5,7},{6,8},{7,9},{8,10},{9,11},{10,... | collective-permute-start | bytes 196616 | tf_op jit(solution)/shard_map/ppermute | solution.py:23
  18.1 24.2 %collective-permute-start.7 = (bf16[64,512]{1,0:T(8,128)(2,1)}, bf16[64,512]{1,0:T(8,128)(2,1)}, u32[]{:S(2)}, u32[]{:S(2)}) collective-permute-start(bf16[64,512]{1,0:T(8,128)(2,1)} %param.16), channel_id=1, source_target_pairs={{0,1},{1,2},{2,3},{3,4},{4,5},{5,6},{6,7},{7,8},{8,9},{9,10},{10,1... | collective-permute-start | bytes 196616 | tf_op jit(solution)/shard_map/ppermute | solution.py:23
  20.7 24.1 %collective-permute-start = (bf16[64,512]{1,0:T(8,128)(2,1)}, bf16[64,512]{1,0:T(8,128)(2,1)}, u32[]{:S(2)}, u32[]{:S(2)}) collective-permute-start(bf16[64,512]{1,0:T(8,128)(2,1)} %param.17), channel_id=1, source_target_pairs={{0,4},{1,5},{2,6},{3,7},{4,8},{5,9},{6,10},{7,11},{8,12},{9,13},{1... | collective-permute-start | bytes 196616 | tf_op jit(solution)/shard_map/ppermute | solution.py:23
  30.2 0.6 copy-start.6
  30.8 14.8 %collective-permute-start.1 = (bf16[64,512]{1,0:T(8,128)(2,1)}, bf16[64,512]{1,0:T(8,128)(2,1)}, u32[]{:S(2)}, u32[]{:S(2)}) collective-permute-start(bf16[64,512]{1,0:T(8,128)(2,1)} %param.17), channel_id=1, source_target_pairs={{0,3},{1,4},{2,5},{3,6},{4,7},{5,8},{6,9},{7,10},{8,11},{9,12},{10... | collective-permute-start | bytes 196616 | tf_op jit(solution)/shard_map/ppermute | solution.py:23
  35.3 11.2 %collective-permute-start.2 = (bf16[64,512]{1,0:T(8,128)(2,1)}, bf16[64,512]{1,0:T(8,128)(2,1)}, u32[]{:S(2)}, u32[]{:S(2)}) collective-permute-start(bf16[64,512]{1,0:T(8,128)(2,1)} %param.17), channel_id=1, source_target_pairs={{0,2},{1,3},{2,4},{3,5},{4,6},{5,7},{6,8},{7,9},{8,10},{9,11},{10,... | collective-permute-start | bytes 196616 | tf_op jit(solution)/shard_map/ppermute | solution.py:23
  39.5 7.8 %collective-permute-start.3 = (bf16[64,512]{1,0:T(8,128)(2,1)}, bf16[64,512]{1,0:T(8,128)(2,1)}, u32[]{:S(2)}, u32[]{:S(2)}) collective-permute-start(bf16[64,512]{1,0:T(8,128)(2,1)} %param.17), channel_id=1, source_target_pairs={{0,1},{1,2},{2,3},{3,4},{4,5},{5,6},{6,7},{7,8},{8,9},{9,10},{10,1... | collective-permute-start | bytes 196616 | tf_op jit(solution)/shard_map/ppermute | solution.py:23
  49.0 1.9 copy-start.4
  52.4 29.1 %copy-start.9 = (f32[1536]{0:T(1024)S(1)}, f32[1536]{0:T(1024)}, u32[]{:S(2)}) copy-start(f32[1536]{0:T(1024)} %param.21) | copy-start | bytes 18436
  80.6 0.8 copy-start.2
  182.3 32.0 %all-to-all-start.2 = ((bf16[1,128,8,4,128]{4,3,2,0,1:T(4,128)(2,1)}), bf16[1,128,8,4,128]{4,3,2,0,1:T(4,128)(2,1)}, u32[]{:S(2)}, u32[]{:S(2)}) async-start(bf16[1,128,8,4,128]{4,3,2,0,1:T(4,128)(2,1)} %bitcast.80), calls=%async_computation.2 | async-start | bytes 2097152 | tf_op jit(solution)/shard_map/all_to_all | solution.py:57
  187.3 115.2 %all-gather.8.cloned.1.call-start = ((), (), s32[]{:S(2)}) async-start(), calls=%async_computation.5 | async-start | bytes 3244032 | tf_op jit(solution)/shard_map/all_gather | solution.py:105
  197.3 22.0 %copy-start.8 = (s32[64,6]{0,1:T(8,128)S(1)}, s32[64,6]{0,1:T(8,128)}, u32[]{:S(2)}) copy-start(s32[64,6]{0,1:T(8,128)} %param.22) | copy-start | bytes 4612
  197.3 22.5 %copy-start.7 = (f32[64,6]{0,1:T(8,128)S(1)}, f32[64,6]{0,1:T(8,128)}, u32[]{:S(2)}) copy-start(f32[64,6]{0,1:T(8,128)} %param.23) | copy-start | bytes 4612
  197.3 23.3 %copy-start.10 = (s32[32]{0:T(128)S(1)}, s32[32]{0:T(128)}, u32[]{:S(2)}) copy-start(s32[32]{0:T(128)} %param.29) | copy-start | bytes 388
  214.3 68.7 %all-to-all-start.1 = ((bf16[32,4,6,1536]{3,1,2,0:T(4,128)(2,1)}), bf16[32,4,6,1536]{3,1,2,0:T(4,128)(2,1)S(1)}, u32[]{:S(2)}, u32[]{:S(2)}) async-start(bf16[32,4,6,1536]{3,1,2,0:T(4,128)(2,1)} %copy.90), calls=%async_computation.1 | async-start | bytes 4718592 | tf_op jit(solution)/shard_map/all_to_all | solution.py:133
  298.5 4.0 %copy-start.3 = (f32[64,1536]{1,0:T(8,128)S(1)}, f32[64,1536]{1,0:T(8,128)}, u32[]{:S(2)}) copy-start(f32[64,1536]{1,0:T(8,128)} %copy-done.2) | copy-start | bytes 1179652
  298.5 7.4 %copy-start.1 = (bf16[4,256,1536]{2,1,0:T(8,128)(2,1)S(1)}, bf16[4,256,1536]{2,1,0:T(8,128)(2,1)}, u32[]{:S(2)}) copy-start(bf16[4,256,1536]{2,1,0:T(8,128)(2,1)} %param.27) | copy-start | bytes 9437188
Sparse Core Ops, SparseCore 0:
  10.9 65.6 all-gather.3
  79.4 91.6 all-gather.5
  191.0 72.4 all-gather.7
where the time goes:
time: 317 us; the launch traced here: 312 us
  waiting for transfers between devices  91.7 us (29%)
  blocking collectives  80.8 us (25%)
  local copies, waits for them, and re-layouts  51.1 us (16%)
  starting transfers between devices  34.6 us (11%)
  matrix products  21 us (7%)
  other arithmetic  19.2 us (6%)
  between operations  14.1 us (4%)
    all_to_all x1, blocking collectives, shards(): lax.all_to_all(outgoing, 'seq', split_axis=0, concat_axis=0, tiled=True)  80.8 us
    all_to_all x1, waiting for transfers between devices, shards(): lax.all_to_all(half_out, 'seq', split_axis=0, concat_axis=0, tiled=True)  48.6 us
    ppermute x8, starting transfers between devices, from_behind(): return lax.ppermute(shard, axis, pairs)  24.4 us
    all_gather x1, waiting for transfers between devices, shards(): lax.all_gather(out_weight, 'seq', axis=1, tiled=True)  24.2 us
    all_to_all x1, waiting for transfers between devices, shards(): lax.all_to_all(cache_blocks, 'seq', split_axis=1, concat_axis=0, tiled=True)  17 us
    unnamed x33, local copies, waits for them, and re-layouts  10.5 us
    scatter x1, other arithmetic, shards(): outgoing.at[jnp.concatenate([first_slot, second_slot])]  9.06 us
    reshape x2, local copies, waits for them, and re-layouts, shards(): outgoing.reshape(HALVES // local_halves, local_halves, CAP, width_model)  8.06 us
  transfers between devices with their start and end apart: 13, of which 3 were waited for; matrix products, arithmetic and copies ran while one was open for 28% of the time, Pallas kernels for 0%

commit v1 on v0

--- a/solution.py
+++ b/solution.py
@@ -3,6 +3,8 @@
 import jax
 import jax.numpy as jnp
 from jax import lax
+from jax.experimental import pallas as pl
+from jax.experimental.pallas import tpu as pltpu
 from jax.sharding import PartitionSpec as P
 
 HD = 128
@@ -11,6 +13,9 @@
 REACH = 4
 HALVES = 128
 CAP = 6
+Z_SIZE = 4
+PLANE = 8
+MIB = 1024 * 1024
 
 
 NEGATIVE = -1e30
@@ -37,7 +42,7 @@
     return jnp.dot(shared_act, down_part, preferred_element_type=jnp.float32)
 
 
-def shards(
+def general_shards(
     queries,
     key_vectors,
     value_vectors,
@@ -141,6 +146,364 @@
     return (layer_out, cache_out)
 
 
+VMEM = pl.BlockSpec(memory_space=pltpu.VMEM)
+SMEM = pl.BlockSpec(memory_space=pltpu.SMEM)
+ANY = pl.BlockSpec(memory_space=pl.ANY)
+
+
+def dot_rows(left, right):
+    return lax.dot_general(left, right, (((1,), (1,)), ((), ())), preferred_element_type=jnp.float32)
+
+
+def dot(left, right):
+    return jnp.dot(left, right, preferred_element_type=jnp.float32)
+
+
+def silu_times(gate, up):
+    return (gate / (1.0 + jnp.exp(-gate)) * up).astype(jnp.bfloat16)
+
+
+def attention_kernel(first_ref, lengths_ref, q_ref, k4_ref, k3_ref, k2_ref, k1_ref, own_ref, out_ref):
+    tokens = q_ref.shape[0]
+    kv_width = own_ref.shape[1] // 2
+    kv_heads = kv_width // HD
+    group = q_ref.shape[1] // HD // kv_heads
+    blocks = [k4_ref, k3_ref, k2_ref, k1_ref, own_ref]
+    keys = len(blocks) * tokens
+    first = first_ref[0]
+    query_pos = first + lax.broadcasted_iota(jnp.int32, (tokens, keys), 0)
+    key_pos = first - (keys - tokens) + lax.broadcasted_iota(jnp.int32, (tokens, keys), 1)
+    start = jnp.zeros((tokens, keys), jnp.int32)
+    end = jnp.int32(0)
+    for request in range(lengths_ref.shape[0]):
+        end = end + lengths_ref[request]
+        start = jnp.maximum(start, jnp.where(query_pos >= end, end, 0))
+    hidden = jnp.where((key_pos >= start) & (key_pos <= query_pos), 0.0, NEGATIVE)
+    hidden = jnp.concatenate([hidden] * group, axis=0)
+    scale = 1.0 / math.sqrt(HD)
+    for kv in range(kv_heads):
+        at = slice(kv * HD, (kv + 1) * HD)
+        value_at = slice(kv_width + kv * HD, kv_width + (kv + 1) * HD)
+        key = jnp.concatenate([block[:, at] for block in blocks], axis=0)
+        value = jnp.concatenate([block[:, value_at] for block in blocks], axis=0)
+        heads = [kv * group + member for member in range(group)]
+        query = jnp.concatenate([q_ref[:, h * HD : (h + 1) * HD] for h in heads], axis=0)
+        scores = dot_rows(query, key) * scale + hidden
+        weights = jnp.exp(scores - jnp.max(scores, axis=-1, keepdims=True))
+        total = jnp.sum(weights, axis=-1, keepdims=True)
+        result = (dot(weights.astype(jnp.bfloat16), value) / total).astype(jnp.bfloat16)
+        for member, h in enumerate(heads):
+            out_ref[:, h * HD : (h + 1) * HD] = result[member * tokens : (member + 1) * tokens]
+
+
+def project_kernel(core_ref, mine_ref, other_ref, weight_ref, own_ref, send_ref, *, chunk):
+    tokens = mine_ref.shape[0]
+    heads = jnp.concatenate([mine_ref[...], other_ref[...]], axis=0)
+    turned = dot_rows(weight_ref[...], heads)
+    is_first = core_ref[0] == 0
+    pieces = []
+    for at in range(0, weight_ref.shape[0], chunk):
+        piece = turned[at : at + chunk]
+        pieces.append(jnp.where(is_first, piece, 0.0))
+        pieces.append(jnp.where(is_first, 0.0, piece))
+    out = jnp.concatenate(pieces, axis=0).T
+    own_ref[...] = out[:tokens]
+    send_ref[...] = out[tokens:]
+
+
+def norm_kernel(residual_ref, own_ref, received_ref, gain_ref, mixed_ref, normed_ref):
+    mixed = residual_ref[...].astype(jnp.float32) + (own_ref[...] + received_ref[...])
+    mixed_ref[...] = mixed
+    mean_square = jnp.mean(mixed * mixed, axis=-1, keepdims=True)
+    normed = (mixed * lax.rsqrt(mean_square + EPSILON) * gain_ref[...]).astype(jnp.bfloat16)
+    for z in range(normed_ref.shape[0]):
+        normed_ref[z] = normed
+
+
+def pick_kernel(code_ref, rows_ref, out_ref):
+    _, picked, _ = out_ref.shape
+    tokens = rows_ref.shape[0]
+    row = pl.program_id(0) * picked + lax.broadcasted_iota(jnp.int32, (picked, tokens), 0)
+    chosen = code_ref[0:1, :] == row
+    for choice in range(1, TOP):
+        chosen = chosen | (code_ref[choice : choice + 1, :] == row)
+    onehot = jnp.where(chosen, 1.0, 0.0).astype(jnp.bfloat16)
+    out_ref[0] = dot(onehot, rows_ref[...]).astype(jnp.bfloat16)
+
+
+def shared_kernel(code_ref, prob_ref, rows_ref, gate_up_ref, down_ref, out_ref, mix_ref):
+    parts = gate_up_ref.shape[0]
+    gate_weight = jnp.concatenate([gate_up_ref[p, 0] for p in range(parts)], axis=0)
+    up_weight = jnp.concatenate([gate_up_ref[p, 1] for p in range(parts)], axis=0)
+    rows = rows_ref[...]
+    act = silu_times(dot_rows(rows, gate_weight), dot_rows(rows, up_weight))
+    out_ref[...] = dot(act, down_ref[...])
+    column = lax.broadcasted_iota(jnp.int32, mix_ref.shape, 1)
+    mix = jnp.zeros(mix_ref.shape, jnp.float32)
+    for choice in range(TOP):
+        one = slice(choice, choice + 1)
+        mix = jnp.where(code_ref[:, one] == column, prob_ref[:, one], mix)
+    mix_ref[...] = mix.astype(jnp.bfloat16)
+
+
+def experts_kernel(rows_ref, gate_up_ref, down_ref, out_ref):
+    sources, both, width = rows_ref.shape
+    per_half = both // 2
+    rows = rows_ref[...].astype(jnp.float32)
+    results = []
+    for half in range(2):
+        own = rows[:, half * per_half : (half + 1) * per_half]
+        own = own.reshape(sources * per_half, width).astype(jnp.bfloat16)
+        act = silu_times(dot(own, gate_up_ref[half, 0]), dot(own, gate_up_ref[half, 1]))
+        results.append(dot(act, down_ref[half]).reshape(sources, per_half, width))
+    out_ref[...] = jnp.concatenate(results, axis=1).astype(jnp.bfloat16)
+
+
+def combine_kernel(mix_ref, rows_ref, shared_ref, out_ref):
+    out_ref[...] = (dot(mix_ref[...], rows_ref[...]) + shared_ref[...]).astype(jnp.bfloat16)
+
+
+def final_kernel(mixed_ref, parts_ref, out_ref):
+    total = mixed_ref[...]
+    for z in range(parts_ref.shape[0]):
+        total = total + parts_ref[z].astype(jnp.float32)
+    out_ref[...] = total.astype(jnp.bfloat16)
+
+
+def reorder_kernel(table_ref, from_ref, to_ref, sems):
+    copies = []
+    for block in range(to_ref.shape[0]):
+        copy = pltpu.make_async_copy(from_ref.at[table_ref[block]], to_ref.at[block], sems.at[block])
+        copy.start()
+        copies.append(copy)
+    for copy in copies:
+        copy.wait()
+
+
+def params(mib):
+    return pltpu.CompilerParams(vmem_limit_bytes=mib * MIB)
+
+
+def cost(flops, moved):
+    return pl.CostEstimate(flops=int(flops), bytes_accessed=int(moved), transcendentals=0)
+
+
+def route_codes(route_ids, z_index):
+    tokens = route_ids.shape[0]
+    experts = jnp.arange(EXPERTS, dtype=jnp.int32)
+    named = route_ids[:, :, None] == experts[None, None, :]
+    member = jnp.any(named, axis=1).astype(jnp.float32)
+    order = jnp.arange(tokens, dtype=jnp.int32)
+    before = (order[None, :] < order[:, None]).astype(jnp.float32)
+    ahead = dot(before, member)
+    rank = jnp.sum(jnp.where(named, ahead[:, None, :], 0.0), axis=2).astype(jnp.int32)
+    half_experts = EXPERTS // 2
+    per_device = half_experts // PLANE
+    plane_at = (route_ids % half_experts) // per_device
+    in_device = (route_ids % per_device) * Z_SIZE + z_index
+    code = (plane_at * per_device * Z_SIZE + in_device) * CAP + rank
+    return code + (route_ids // half_experts) * (PLANE * per_device * Z_SIZE * CAP)
+
+
+def shards(
+    queries,
+    key_vectors,
+    value_vectors,
+    lengths,
+    out_weight,
+    residual,
+    norm_gain,
+    route_ids,
+    route_logits,
+    shared_gate_up,
+    shared_down,
+    expert_gate_up,
+    expert_down,
+    cache_blocks,
+    block_table,
+):
+    tokens, width = residual.shape
+    devices = lax.axis_size("seq")
+    me = lax.axis_index("seq")
+    z_index = me // PLANE
+    z_groups = [[p + PLANE * z for z in range(Z_SIZE)] for p in range(PLANE)]
+    planes = [[p + PLANE * z for p in range(PLANE)] for z in range(Z_SIZE)]
+    same_core = [[core + 2 * chip for chip in range(devices // 2)] for core in range(2)]
+    partner = [(i, i ^ 1) for i in range(devices)]
+    bf16, f32 = jnp.bfloat16, jnp.float32
+    shape = jax.ShapeDtypeStruct
+
+    turned_weight = lax.all_gather(
+        out_weight.T, "seq", axis=0, tiled=True, axis_index_groups=same_core
+    )
+
+    own_kv = jnp.concatenate([key_vectors, value_vectors], axis=1)
+    behind = [from_behind(own_kv, "seq", offset) for offset in range(REACH, 0, -1)]
+
+    _, block_tokens, layers, kv_heads, head_size = cache_blocks.shape
+    per_device = block_tokens // devices
+    outgoing_cache = cache_blocks.reshape(devices, per_device * layers, kv_heads, head_size)
+    handed = lax.all_to_all(outgoing_cache, "seq", split_axis=0, concat_axis=0, tiled=True)
+    cache_out = pl.pallas_call(
+        reorder_kernel,
+        out_shape=shape(handed.shape, bf16),
+        in_specs=[SMEM, ANY],
+        out_specs=ANY,
+        scratch_shapes=[pltpu.SemaphoreType.DMA((devices,))],
+        cost_estimate=cost(0, 2 * handed.size * 2),
+        name="reorder",
+    )(block_table, handed)
+    cache_out = cache_out.reshape(devices, per_device, layers, kv_heads, head_size)
+
+    code = route_codes(route_ids, z_index).astype(f32)
+    probs = jax.nn.softmax(route_logits, axis=-1)
+    pad = ((0, 0), (0, 2))
+    packed = jnp.concatenate([jnp.pad(code, pad), jnp.pad(probs, pad)], axis=1).T
+    packed = lax.all_gather(packed, "seq", axis=0, axis_index_groups=z_groups)
+    gathered_codes = packed[:, :8].astype(jnp.int32) - (z_index % 2) * (PLANE * 4 * Z_SIZE * CAP)
+    all_tokens = Z_SIZE * tokens
+    code_rows = jnp.transpose(gathered_codes, (1, 0, 2)).reshape(8, all_tokens)
+    code_columns = jnp.transpose(gathered_codes, (0, 2, 1)).reshape(all_tokens, 8)
+    prob_columns = jnp.transpose(packed[:, 8:], (0, 2, 1)).reshape(all_tokens, 8)
+
+    shared_both = lax.all_gather(
+        jnp.transpose(shared_gate_up, (1, 2, 0)), "seq", axis=0, axis_index_groups=planes
+    )
+    shared_back = lax.all_gather(
+        shared_down, "seq", axis=0, tiled=True, axis_index_groups=planes
+    )
+
+    first_token = jnp.reshape(me * tokens, (1,)).astype(jnp.int32)
+    heads = pl.pallas_call(
+        attention_kernel,
+        out_shape=shape((tokens, width), bf16),
+        in_specs=[SMEM, SMEM] + [VMEM] * 6,
+        out_specs=VMEM,
+        compiler_params=params(24),
+        cost_estimate=cost(4 * tokens * 5 * tokens * width, 2 * MIB),
+        name="attention",
+    )(first_token, lengths, queries, *behind, own_kv)
+
+    other_heads = lax.ppermute(heads, "seq", partner)
+    core = jnp.reshape(me % 2, (1,)).astype(jnp.int32)
+    steps = 4
+    half_columns = turned_weight.shape[0]
+    own_out, other_out = pl.pallas_call(
+        lambda *refs: project_kernel(*refs, chunk=out_weight.shape[1]),
+        grid=(steps,),
+        out_shape=[shape((tokens, width), f32)] * 2,
+        in_specs=[
+            SMEM,
+            pl.BlockSpec((tokens, width), lambda i: (0, 0)),
+            pl.BlockSpec((tokens, width), lambda i: (0, 0)),
+            pl.BlockSpec((half_columns // steps, width), lambda i: (i, 0)),
+        ],
+        out_specs=[pl.BlockSpec((tokens, width // steps), lambda i: (0, i))] * 2,
+        compiler_params=params(24),
+        cost_estimate=cost(4 * tokens * width * half_columns, 3 * MIB),
+        name="project",
+    )(core, heads, other_heads, turned_weight)
+    received_out = lax.ppermute(other_out, "seq", partner)
+
+    mixed, normed = pl.pallas_call(
+        norm_kernel,
+        out_shape=[shape((tokens, width), f32), shape((Z_SIZE, tokens, width), bf16)],
+        in_specs=[VMEM] * 4,
+        out_specs=[VMEM] * 2,
+        compiler_params=params(16),
+        cost_estimate=cost(8 * tokens * width, 2 * MIB),
+        name="norm",
+    )(residual, own_out, received_out, norm_gain.reshape(1, width))
+
+    rows = lax.all_to_all(
+        normed, "seq", split_axis=0, concat_axis=0, tiled=True, axis_index_groups=z_groups
+    ).reshape(all_tokens, width)
+
+    local_halves, _, _, half_ff = expert_gate_up.shape
+    per_half = Z_SIZE * CAP
+    picked = local_halves * per_half
+    outgoing = pl.pallas_call(
+        pick_kernel,
+        grid=(PLANE,),
+        out_shape=shape((PLANE, picked, width), bf16),
+        in_specs=[
+            pl.BlockSpec((8, all_tokens), lambda i: (0, 0)),
+            pl.BlockSpec((all_tokens, width), lambda i: (0, 0)),
+        ],
+        out_specs=pl.BlockSpec((1, picked, width), lambda i: (i, 0, 0)),
+        compiler_params=params(16),
+        cost_estimate=cost(2 * PLANE * picked * all_tokens * width, 3 * MIB),
+        name="pick",
+    )(code_rows, rows)
+
+    arrived = lax.all_to_all(
+        outgoing, "seq", split_axis=0, concat_axis=0, tiled=True, axis_index_groups=planes
+    )
+    shared_part, mix = pl.pallas_call(
+        shared_kernel,
+        out_shape=[shape((all_tokens, width), f32), shape((all_tokens, PLANE * picked), bf16)],
+        in_specs=[VMEM] * 5,
+        out_specs=[VMEM] * 2,
+        compiler_params=params(32),
+        cost_estimate=cost(6 * all_tokens * 256 * width, 5 * MIB),
+        name="shared_expert",
+    )(code_columns, prob_columns, rows, shared_both, shared_back)
+
+    gate_up = jnp.transpose(expert_gate_up, (0, 2, 1, 3))
+    returning = pl.pallas_call(
+        experts_kernel,
+        grid=(local_halves // 2,),
+        out_shape=shape((PLANE, picked, width), bf16),
+        in_specs=[
+            pl.BlockSpec((PLANE, 2 * per_half, width), lambda i: (0, i, 0)),
+            pl.BlockSpec((2, 2, width, half_ff), lambda i: (i, 0, 0, 0)),
+            pl.BlockSpec((2, half_ff, width), lambda i: (i, 0, 0)),
+        ],
+        out_specs=pl.BlockSpec((PLANE, 2 * per_half, width), lambda i: (0, i, 0)),
+        compiler_params=params(40),
+        cost_estimate=cost(6 * PLANE * picked * half_ff * width, 14 * MIB),
+        name="experts",
+    )(arrived, gate_up, expert_down)
+    returned = lax.all_to_all(
+        returning, "seq", split_axis=0, concat_axis=0, tiled=True, axis_index_groups=planes
+    ).reshape(PLANE * picked, width)
+
+    column_steps = 2
+    part_width = width // column_steps
+    parts = pl.pallas_call(
+        combine_kernel,
+        grid=(column_steps,),
+        out_shape=shape((all_tokens, width), bf16),
+        in_specs=[
+            pl.BlockSpec((all_tokens, PLANE * picked), lambda i: (0, 0)),
+            pl.BlockSpec((PLANE * picked, part_width), lambda i: (0, i)),
+            pl.BlockSpec((all_tokens, part_width), lambda i: (0, i)),
+        ],
+        out_specs=pl.BlockSpec((all_tokens, part_width), lambda i: (0, i)),
+        compiler_params=params(24),
+        cost_estimate=cost(2 * all_tokens * PLANE * picked * width, 5 * MIB),
+        name="combine",
+    )(mix, returned, shared_part)
+    parts = lax.all_to_all(
+        parts.reshape(Z_SIZE, tokens, width),
+        "seq",
+        split_axis=0,
+        concat_axis=0,
+        tiled=True,
+        axis_index_groups=z_groups,
+    )
+    layer_out = pl.pallas_call(
+        final_kernel,
+        out_shape=shape((tokens, width), bf16),
+        in_specs=[VMEM] * 2,
+        out_specs=VMEM,
+        compiler_params=params(16),
+        cost_estimate=cost(5 * tokens * width, MIB),
+        name="final",
+    )(mixed, parts)
+    return (layer_out, cache_out)
+
+
 def solution(mesh):
     in_specs = (
         P("seq", "head"),
@@ -160,4 +523,6 @@
         P(),
     )
     out_specs = (P(("seq", "head"), None), P(None, "seq", None, "head", None))
-    return jax.shard_map(shards, mesh=mesh, in_specs=in_specs, out_specs=out_specs, check_vma=False)
+    planes_fit = mesh.shape["seq"] == Z_SIZE * PLANE and mesh.shape["head"] == 1
+    body = shards if planes_fit else general_shards
+    return jax.shard_map(body, mesh=mesh, in_specs=in_specs, out_specs=out_specs, check_vma=False)

time: 317 us -> 270 us (0.85)
  Pallas kernels: 0 us -> 48.9 us
  blocking collectives: 80.8 us -> 40.4 us
  local copies, waits for them, and re-layouts: 51.1 us -> 21 us
  matrix products: 21 us -> 0.13 us
  other arithmetic: 19.2 us -> 0.44 us
  waiting for transfers between devices: 91.7 us -> 106 us
    all_to_all x1 -> x0, blocking collectives: 80.8 us -> none  [shards(): lax.all_to_all(outgoing, 'seq', split_axis=0, concat_axis=0, tiled=True)]
    pallas_call x0 -> x9, Pallas kernels: none -> 48.9 us  [the longest x1 33.8 us: shards(): pl.pallas_call(reorder_kernel, out_shape=shape(handed.shape, bf16), in_sp...]
    all_gather x0 -> x2, blocking collectives: none -> 40.4 us  [the longest x1 24.3 us: shards(): packed = lax.all_gather(packed, 'seq', axis=0, axis_index_groups=z_groups)]
    dot_general x7 -> x1, matrix products: 21 us -> 0.13 us  [dot(): return jnp.dot(left, right, preferred_element_type=jnp.float32)]
    all_gather x3 -> x2, waiting for transfers between devices: 24.2 us -> 43.7 us  [the longest x1 43.7 us: shards(): lax.all_gather(out_weight.T, 'seq', axis=0, tiled=True, axis_index_groups...]
    reshape x8 -> x2, local copies, waits for them, and re-layouts: 16.1 us -> 0.09 us  [the longest x1 0.08 us: shards(): code_rows = jnp.transpose(gathered_codes, (1, 0, 2)).reshape(8, all_tokens)]
    all_to_all x2 -> x5, starting transfers between devices: 9.98 us -> 23.5 us  [the longest x1 5.56 us: shards(): lax.all_to_all(outgoing_cache, 'seq', split_axis=0, concat_axis=0, tiled=...]
    ppermute x8 -> x4, starting transfers between devices: 24.4 us -> 12 us  [from_behind(): return lax.ppermute(shard, axis, pairs)]
  transfers between devices with their start and end apart: 13 -> 13, of which waited for: 3 -> 8; matrix products, arithmetic and copies ran while one was open for 28% -> 3% of each run, Pallas kernels for 0% -> 15%
where the time goes in v1:
time: 270 us; the launch traced here: 268 us
  waiting for transfers between devices  106 us (39%)
  Pallas kernels  48.9 us (18%)
  blocking collectives  40.4 us (15%)
  starting transfers between devices  35.6 us (13%)
  local copies, waits for them, and re-layouts  21 us (8%)
  between operations  15.8 us (6%)
    all_gather x1, waiting for transfers between devices, shards(): lax.all_gather(out_weight.T, 'seq', axis=0, tiled=True, axis_index_groups...  43.7 us
    pallas_call x1, Pallas kernels, shards(): pl.pallas_call(reorder_kernel, out_shape=shape(handed.shape, bf16), in_sp...  33.8 us
    all_to_all x1, waiting for transfers between devices, shards(): lax.all_to_all(returning, 'seq', split_axis=0, concat_axis=0, tiled=True,...  29.5 us
    all_gather x1, blocking collectives, shards(): packed = lax.all_gather(packed, 'seq', axis=0, axis_index_groups=z_groups)  24.3 us
    all_to_all x1, waiting for transfers between devices, shards(): lax.all_to_all(outgoing, 'seq', split_axis=0, concat_axis=0, tiled=True,...  21.7 us
    unnamed x34, local copies, waits for them, and re-layouts  20 us
    all_gather x1, blocking collectives, shards(): lax.all_gather(shared_down, 'seq', axis=0, tiled=True, axis_index_groups=...  16.1 us
    ppermute x4, starting transfers between devices, from_behind(): return lax.ppermute(shard, axis, pairs)  12 us
  transfers between devices with their start and end apart: 13, of which 8 were waited for; matrix products, arithmetic and copies ran while one was open for 3% of the time, Pallas kernels for 15%

profile of v1, /device:TPU:10, one launch (start us, length us, event | category | flops | bytes accessed | tf_op | source)
XLA Modules:
  0.0 268.5 jit_solution(12872955733430590879)
XLA Ops:
  10.5 3.4 %collective-permute-start = (bf16[64,1024]{1,0:T(8,128)(2,1)S(1)}, bf16[64,1024]{1,0:T(8,128)(2,1)S(1)}, u32[]{:S(2)}, u32[]{:S(2)}) collective-permute-start(bf16[64,1024]{1,0:T(8,128)(2,1)S(1)} %constant_dynamic-update-slice_fusion.own_ref), channel_id=1, source_target_pairs={{0,4},{1,5},{2,6},{3,7},{4,8},{5,9},{6,10},{7,11},{8,12},{9,13},{1... | collective-permute-start | bytes 393224 | tf_op jit(solution)/shard_map/ppermute | solution.py:28
  13.9 2.6 collective-permute-start.1
  16.5 3.4 %collective-permute-start.2 = (bf16[64,1024]{1,0:T(8,128)(2,1)S(1)}, bf16[64,1024]{1,0:T(8,128)(2,1)S(1)}, u32[]{:S(2)}, u32[]{:S(2)}) collective-permute-start(bf16[64,1024]{1,0:T(8,128)(2,1)S(1)} %constant_dynamic-update-slice_fusion.own_ref), channel_id=1, source_target_pairs={{0,2},{1,3},{2,4},{3,5},{4,6},{5,7},{6,8},{7,9},{8,10},{9,11},{10,... | collective-permute-start | bytes 393224 | tf_op jit(solution)/shard_map/ppermute | solution.py:28
  19.9 2.6 collective-permute-start.3
  22.5 3.2 %collective-permute-done.2.k2_ref = bf16[64,1024]{1,0:T(8,128)(2,1)S(1)} collective-permute-done((bf16[64,1024]{1,0:T(8,128)(2,1)S(1)}, bf16[64,1024]{1,0:T(8,128)(2,1)S(1)}, u32[]{:S(2)}, u32[]{:S(2)}) %collective-permute-start.2) | collective-permute-done | bytes 131104 | tf_op jit(solution)/shard_map/ppermute | solution.py:28
  28.8 1.8 attention.1.refs_1_
  32.1 43.7 %all-gather.5.cloned.1.call-done.refs_3_ = bf16[768,1536]{1,0:T(8,128)(2,1)} async-done(((bf16[48,1536]{1,0:T(8,128)(2,1)}), bf16[768,1536]{1,0:T(8,128)(2,1)}) %all-gather.5.cloned.1.call-update) | async-done | bytes 2359312 | tf_op jit(solution)/shard_map/all_gather | solution.py:336
  82.8 3.6 %all-to-all-start = ((bf16[4,64,1536]{2,1,0:T(8,128)(2,1)}), bf16[4,64,1536]{2,1,0:T(8,128)(2,1)S(1)}, u32[]{:S(2)}, u32[]{:S(2)}) async-start(bf16[4,64,1536]{2,1,0:T(8,128)(2,1)} %get-tuple-element.11), calls=%async_computation | async-start | bytes 1572864 | tf_op jit(solution)/shard_map/all_to_all | solution.py:418
  86.9 24.3 %all-gather = f32[64,64]{1,0:T(8,128)S(1)} all-gather(f32[16,64]{1,0:T(8,128)S(1)} %fusion.2), channel_id=2, replica_groups={{0,8,16,24},{1,9,17,25},{2,10,18,26},{3,11,19,27},{4,12,20,28},{5,13,21..., dimensions={0}, use_global_device_ids=true | all-gather | bytes 20480 | tf_op jit(solution)/shard_map/all_gather | solution.py:362
  111.3 2.3 pick.1
  115.0 4.1 %all-to-all-start.1 = ((bf16[8,96,1536]{2,1,0:T(8,128)(2,1)}), bf16[8,96,1536]{2,1,0:T(8,128)(2,1)S(1)}, u32[]{:S(2)}, u32[]{:S(2)}) async-start(bf16[8,96,1536]{2,1,0:T(8,128)(2,1)} %copy-done.1), calls=%async_computation.1 | async-start | bytes 4718592 | tf_op jit(solution)/shard_map/all_to_all | solution.py:439
  119.1 6.3 %copy.37 = bf16[4,1536,2,256]{3,1,2,0:T(8,128)(2,1)} copy(bf16[4,1536,2,256]{3,2,1,0:T(2,128)(2,1)} %param.26) | data formatting | bytes 12582912 | tf_op args[11]
  125.4 21.7 %all-to-all-done.1.rows_ref = bf16[8,96,1536]{2,1,0:T(8,128)(2,1)S(1)} async-done(((bf16[8,96,1536]{2,1,0:T(8,128)(2,1)}), bf16[8,96,1536]{2,1,0:T(8,128)(2,1)S(1)}, u32[]{:S(2)}, u32[]{:S(2)}) %all-to-all-start.1) | async-done | bytes 2359328 | tf_op jit(solution)/shard_map/all_to_all | solution.py:439
  147.1 2.8 %copy-done = bf16[4,1536,2,256]{3,1,2,0:T(8,128)(2,1)S(1)} copy-done((bf16[4,1536,2,256]{3,1,2,0:T(8,128)(2,1)S(1)}, bf16[4,1536,2,256]{3,1,2,0:T(8,128)(2,1)}, u32[]{:S(2)}) %copy-start) | copy-done | bytes 6291480
  149.9 1.9 copy-done.2
  151.7 3.9 %experts.1 = bf16[8,96,1536]{2,1,0:T(8,128)(2,1)} custom-call(bf16[8,96,1536]{2,1,0:T(8,128)(2,1)S(1)} %all-to-all-done.1.rows_ref, bf16[4,2,1536,256]{3,2,1,0:T(8,128)(2,1)S(1)} %bitcast.26, bf16[4,256,1536]{2,1,0:T(8,128)(2,1)S(1)} %copy-done.2), custom_call_target="tpu_custom_call" | custom-call | flops 1811939328 | bytes 14680064 | tf_op jit(solution)/shard_map/experts/pallas_call | solution.py:453
  155.6 5.0 %all-to-all-start.2 = ((bf16[8,96,1536]{2,1,0:T(8,128)(2,1)}), bf16[8,96,1536]{2,1,0:T(8,128)(2,1)S(1)}, u32[]{:S(2)}, u32[]{:S(2)}) async-start(bf16[8,96,1536]{2,1,0:T(8,128)(2,1)} %experts.1), calls=%async_computation.2 | async-start | bytes 4718592 | tf_op jit(solution)/shard_map/all_to_all | solution.py:467
  161.2 29.5 %all-to-all-done.2 = bf16[8,96,1536]{2,1,0:T(8,128)(2,1)S(1)} async-done(((bf16[8,96,1536]{2,1,0:T(8,128)(2,1)}), bf16[8,96,1536]{2,1,0:T(8,128)(2,1)S(1)}, u32[]{:S(2)}, u32[]{:S(2)}) %all-to-all-start.2) | async-done | bytes 2359328 | tf_op jit(solution)/shard_map/all_to_all | solution.py:467
  190.7 5.6 %all-to-all-start.4 = ((bf16[32,32,4,128]{3,2,1,0:T(4,128)(2,1)}), bf16[32,32,4,128]{3,2,1,0:T(4,128)(2,1)}, u32[]{:S(2)}, u32[]{:S(2)}) async-start(bf16[32,32,4,128]{3,2,1,0:T(4,128)(2,1)} %bitcast.34), calls=%async_computation.4 | async-start | bytes 2097152 | tf_op jit(solution)/shard_map/all_to_all | solution.py:346
  196.5 16.1 %all_gather.23.down_ref = bf16[256,1536]{1,0:T(8,128)(2,1)} all-gather(bf16[32,1536]{1,0:T(8,128)(2,1)S(1)} %copy-done.11), channel_id=1, replica_groups={{0,1,2,3,4,5,6,7},{8,9,10,11,12,13,14,15},{16,17,18,19,20,21,22,23},{24..., dimensions={0}, use_global_device_ids=true | all-gather | bytes 884736 | tf_op jit(solution)/shard_map/all_gather | solution.py:372
  216.7 2.0 combine.1
  218.7 2.4 all-to-all-done.4.from_ref
  221.2 5.2 %all-to-all-start.3 = ((bf16[4,64,1536]{2,1,0:T(8,128)(2,1)}), bf16[4,64,1536]{2,1,0:T(8,128)(2,1)S(1)}, u32[]{:S(2)}, u32[]{:S(2)}) async-start(bf16[4,64,1536]{2,1,0:T(8,128)(2,1)} %bitcast.15), calls=%async_computation.3 | async-start | bytes 1572864 | tf_op jit(solution)/shard_map/all_to_all | solution.py:487
  226.4 33.8 %reorder.1 = bf16[32,32,4,128]{3,2,1,0:T(4,128)(2,1)} custom-call(s32[32]{0:T(128)} %table_ref.1, bf16[32,32,4,128]{3,2,1,0:T(4,128)(2,1)} %all-to-all-done.4.from_ref), custom_call_target="tpu_custom_call" | custom-call | bytes 2097152 | tf_op jit(solution)/shard_map/reorder/pallas_call | solution.py:347
  (63 shorter events, 21.5 us)
Async XLA Ops:
  8.0 71.3 %copy-start.14 = (f32[1536]{0:T(1024)S(1)}, f32[1536]{0:T(1024)}, u32[]{:S(2)}) copy-start(f32[1536]{0:T(1024)} %param.21) | copy-start | bytes 18436
  8.0 71.3 %copy-start.13 = (f32[64,6]{0,1:T(8,128)S(1)}, f32[64,6]{0,1:T(8,128)}, u32[]{:S(2)}) copy-start(f32[64,6]{0,1:T(8,128)} %param.23) | copy-start | bytes 4612
  8.0 71.3 %copy-start.12 = (s32[64,6]{0,1:T(8,128)S(1)}, s32[64,6]{0,1:T(8,128)}, u32[]{:S(2)}) copy-start(s32[64,6]{0,1:T(8,128)} %param.22) | copy-start | bytes 4612
  8.0 73.0 %copy-start.9 = (bf16[64,1536]{1,0:T(8,128)(2,1)S(1)}, bf16[64,1536]{1,0:T(8,128)(2,1)}, u32[]{:S(2)}) copy-start(bf16[64,1536]{1,0:T(8,128)(2,1)} %residual_ref.1) | copy-start | bytes 589828
  8.0 67.8 %all-gather.5.cloned.1.call-start = ((), (), s32[]{:S(2)}) async-start(), calls=%async_computation.5 | async-start | bytes 2506752 | tf_op jit(solution)/shard_map/all_gather | solution.py:336
  10.5 12.0 %collective-permute-start = (bf16[64,1024]{1,0:T(8,128)(2,1)S(1)}, bf16[64,1024]{1,0:T(8,128)(2,1)S(1)}, u32[]{:S(2)}, u32[]{:S(2)}) collective-permute-start(bf16[64,1024]{1,0:T(8,128)(2,1)S(1)} %constant_dynamic-update-slice_fusion.own_ref), channel_id=1, source_target_pairs={{0,4},{1,5},{2,6},{3,7},{4,8},{5,9},{6,10},{7,11},{8,12},{9,13},{1... | collective-permute-start | bytes 393224 | tf_op jit(solution)/shard_map/ppermute | solution.py:28
  13.9 8.6 %collective-permute-start.1 = (bf16[64,1024]{1,0:T(8,128)(2,1)S(1)}, bf16[64,1024]{1,0:T(8,128)(2,1)S(1)}, u32[]{:S(2)}, u32[]{:S(2)}) collective-permute-start(bf16[64,1024]{1,0:T(8,128)(2,1)S(1)} %constant_dynamic-update-slice_fusion.own_ref), channel_id=1, source_target_pairs={{0,3},{1,4},{2,5},{3,6},{4,7},{5,8},{6,9},{7,10},{8,11},{9,12},{10... | collective-permute-start | bytes 393224 | tf_op jit(solution)/shard_map/ppermute | solution.py:28
  16.5 9.3 %collective-permute-start.2 = (bf16[64,1024]{1,0:T(8,128)(2,1)S(1)}, bf16[64,1024]{1,0:T(8,128)(2,1)S(1)}, u32[]{:S(2)}, u32[]{:S(2)}) collective-permute-start(bf16[64,1024]{1,0:T(8,128)(2,1)S(1)} %constant_dynamic-update-slice_fusion.own_ref), channel_id=1, source_target_pairs={{0,2},{1,3},{2,4},{3,5},{4,6},{5,7},{6,8},{7,9},{8,10},{9,11},{10,... | collective-permute-start | bytes 393224 | tf_op jit(solution)/shard_map/ppermute | solution.py:28
  19.9 7.3 %collective-permute-start.3 = (bf16[64,1024]{1,0:T(8,128)(2,1)S(1)}, bf16[64,1024]{1,0:T(8,128)(2,1)S(1)}, u32[]{:S(2)}, u32[]{:S(2)}) collective-permute-start(bf16[64,1024]{1,0:T(8,128)(2,1)S(1)} %constant_dynamic-update-slice_fusion.own_ref), channel_id=1, source_target_pairs={{0,1},{1,2},{2,3},{3,4},{4,5},{5,6},{6,7},{7,8},{8,9},{9,10},{10,1... | collective-permute-start | bytes 393224 | tf_op jit(solution)/shard_map/ppermute | solution.py:28
  30.6 1.5 collective-permute-start.4
  75.8 1.7 copy-start.4
  79.2 1.8 collective-permute-start.5
  82.8 28.4 %all-to-all-start = ((bf16[4,64,1536]{2,1,0:T(8,128)(2,1)}), bf16[4,64,1536]{2,1,0:T(8,128)(2,1)S(1)}, u32[]{:S(2)}, u32[]{:S(2)}) async-start(bf16[4,64,1536]{2,1,0:T(8,128)(2,1)} %get-tuple-element.11), calls=%async_computation | async-start | bytes 1572864 | tf_op jit(solution)/shard_map/all_to_all | solution.py:418
  113.6 1.5 copy-start.1
  115.0 32.0 %all-to-all-start.1 = ((bf16[8,96,1536]{2,1,0:T(8,128)(2,1)}), bf16[8,96,1536]{2,1,0:T(8,128)(2,1)S(1)}, u32[]{:S(2)}, u32[]{:S(2)}) async-start(bf16[8,96,1536]{2,1,0:T(8,128)(2,1)} %copy-done.1), calls=%async_computation.1 | async-start | bytes 4718592 | tf_op jit(solution)/shard_map/all_to_all | solution.py:439
  147.1 2.8 %copy-start = (bf16[4,1536,2,256]{3,1,2,0:T(8,128)(2,1)S(1)}, bf16[4,1536,2,256]{3,1,2,0:T(8,128)(2,1)}, u32[]{:S(2)}) copy-start(bf16[4,1536,2,256]{3,1,2,0:T(8,128)(2,1)} %copy.37) | copy-start | bytes 18874372
  149.9 1.9 copy-start.2
  155.6 35.1 %all-to-all-start.2 = ((bf16[8,96,1536]{2,1,0:T(8,128)(2,1)}), bf16[8,96,1536]{2,1,0:T(8,128)(2,1)S(1)}, u32[]{:S(2)}, u32[]{:S(2)}) async-start(bf16[8,96,1536]{2,1,0:T(8,128)(2,1)} %experts.1), calls=%async_computation.2 | async-start | bytes 4718592 | tf_op jit(solution)/shard_map/all_to_all | solution.py:467
  160.7 35.9 %copy-start.11 = (bf16[32,1536]{1,0:T(8,128)(2,1)S(1)}, bf16[32,1536]{1,0:T(8,128)(2,1)}, u32[]{:S(2)}) copy-start(bf16[32,1536]{1,0:T(8,128)(2,1)} %param.25) | copy-start | bytes 294916
  160.7 52.0 %all-gather.7.cloned.1.call-start = ((), (), s32[]{:S(2)}) async-start(), calls=%async_computation.6 | async-start | bytes 1769472 | tf_op jit(solution)/shard_map/all_gather | solution.py:369
  190.7 30.5 %all-to-all-start.4 = ((bf16[32,32,4,128]{3,2,1,0:T(4,128)(2,1)}), bf16[32,32,4,128]{3,2,1,0:T(4,128)(2,1)}, u32[]{:S(2)}, u32[]{:S(2)}) async-start(bf16[32,32,4,128]{3,2,1,0:T(4,128)(2,1)} %bitcast.34), calls=%async_computation.4 | async-start | bytes 2097152 | tf_op jit(solution)/shard_map/all_to_all | solution.py:346
  213.8 1.4 copy-start.5
  218.7 41.5 %copy-start.7 = (f32[64,1536]{1,0:T(8,128)S(1)}, f32[64,1536]{1,0:T(8,128)}, u32[]{:S(2)}) copy-start(f32[64,1536]{1,0:T(8,128)} %copy-done.6) | copy-start | bytes 1179652
  221.2 39.0 %all-to-all-start.3 = ((bf16[4,64,1536]{2,1,0:T(8,128)(2,1)}), bf16[4,64,1536]{2,1,0:T(8,128)(2,1)S(1)}, u32[]{:S(2)}, u32[]{:S(2)}) async-start(bf16[4,64,1536]{2,1,0:T(8,128)(2,1)} %bitcast.15), calls=%async_computation.3 | async-start | bytes 1572864 | tf_op jit(solution)/shard_map/all_to_all | solution.py:487
  (4 other events, 3.5 us)
Sparse Core Ops, SparseCore 0:
  11.7 64.0 all-gather.4
Sparse Core Ops, SparseCore 1:
  163.0 34.9 all-gather.6

commit v2 on v1

--- a/solution.py
+++ b/solution.py
@@ -163,11 +163,14 @@
     return (gate / (1.0 + jnp.exp(-gate)) * up).astype(jnp.bfloat16)
 
 
-def attention_kernel(first_ref, lengths_ref, q_ref, k4_ref, k3_ref, k2_ref, k1_ref, own_ref, out_ref):
-    tokens = q_ref.shape[0]
+def attention_kernel(
+    first_ref, lengths_ref, q_ref, k4_ref, k3_ref, k2_ref, k1_ref, own_ref, residual_ref, info_ref, out_ref
+):
+    tokens, width = q_ref.shape
+    copies = out_ref.shape[0]
     kv_width = own_ref.shape[1] // 2
     kv_heads = kv_width // HD
-    group = q_ref.shape[1] // HD // kv_heads
+    group = width // HD // kv_heads
     blocks = [k4_ref, k3_ref, k2_ref, k1_ref, own_ref]
     keys = len(blocks) * tokens
     first = first_ref[0]
@@ -181,6 +184,10 @@
     hidden = jnp.where((key_pos >= start) & (key_pos <= query_pos), 0.0, NEGATIVE)
     hidden = jnp.concatenate([hidden] * group, axis=0)
     scale = 1.0 / math.sqrt(HD)
+    part = width // copies
+    for z in range(copies):
+        out_ref[z, :, width : width + part] = residual_ref[:, z * part : (z + 1) * part]
+        out_ref[z, :, width + part :] = info_ref[...]
     for kv in range(kv_heads):
         at = slice(kv * HD, (kv + 1) * HD)
         value_at = slice(kv_width + kv * HD, kv_width + (kv + 1) * HD)
@@ -193,56 +200,64 @@
         total = jnp.sum(weights, axis=-1, keepdims=True)
         result = (dot(weights.astype(jnp.bfloat16), value) / total).astype(jnp.bfloat16)
         for member, h in enumerate(heads):
-            out_ref[:, h * HD : (h + 1) * HD] = result[member * tokens : (member + 1) * tokens]
-
-
-def project_kernel(core_ref, mine_ref, other_ref, weight_ref, own_ref, send_ref, *, chunk):
-    tokens = mine_ref.shape[0]
-    heads = jnp.concatenate([mine_ref[...], other_ref[...]], axis=0)
-    turned = dot_rows(weight_ref[...], heads)
-    is_first = core_ref[0] == 0
-    pieces = []
-    for at in range(0, weight_ref.shape[0], chunk):
-        piece = turned[at : at + chunk]
-        pieces.append(jnp.where(is_first, piece, 0.0))
-        pieces.append(jnp.where(is_first, 0.0, piece))
-    out = jnp.concatenate(pieces, axis=0).T
-    own_ref[...] = out[:tokens]
-    send_ref[...] = out[tokens:]
-
-
-def norm_kernel(residual_ref, own_ref, received_ref, gain_ref, mixed_ref, normed_ref):
-    mixed = residual_ref[...].astype(jnp.float32) + (own_ref[...] + received_ref[...])
-    mixed_ref[...] = mixed
-    mean_square = jnp.mean(mixed * mixed, axis=-1, keepdims=True)
-    normed = (mixed * lax.rsqrt(mean_square + EPSILON) * gain_ref[...]).astype(jnp.bfloat16)
-    for z in range(normed_ref.shape[0]):
-        normed_ref[z] = normed
-
-
-def pick_kernel(code_ref, rows_ref, out_ref):
+            for z in range(copies):
+                out_ref[z, :, h * HD : (h + 1) * HD] = result[member * tokens : (member + 1) * tokens]
+
+
+def project_kernel(heads_ref, residual_ref, weight_ref, out_ref):
+    out = dot_rows(heads_ref[...], weight_ref[...]) + residual_ref[...].astype(jnp.float32)
+    out = out.astype(jnp.bfloat16)
+    for z in range(out_ref.shape[0]):
+        out_ref[z] = out
+
+
+def row_codes(info, first, parity, per_device):
+    where_to = info(first).astype(jnp.int32) - PLANE * parity
+    inside = info(first + 8).astype(jnp.int32)
+    fits = (where_to >= 0) & (where_to < PLANE)
+    return jnp.where(fits, where_to * per_device + inside, -1)
+
+
+def pick_kernel(parity_ref, mixed_ref, gain_ref, info_ref, normed_ref, out_ref, code_ref):
     _, picked, _ = out_ref.shape
-    tokens = rows_ref.shape[0]
+    tokens = normed_ref.shape[0]
+
+    @pl.when(pl.program_id(0) == 0)
+    def _():
+        columns = mixed_ref.shape[2]
+        mixed = [mixed_ref[z].astype(jnp.float32) for z in range(mixed_ref.shape[0])]
+        square = sum(jnp.sum(m * m, axis=-1, keepdims=True) for m in mixed)
+        factor = lax.rsqrt(square / normed_ref.shape[1] + EPSILON)
+        for z, m in enumerate(mixed):
+            at = slice(z * columns, (z + 1) * columns)
+            normed_ref[:, at] = (m * factor * gain_ref[:, at]).astype(jnp.bfloat16)
+        info = info_ref[...].astype(jnp.float32).T
+        code_ref[...] = row_codes(lambda at: info[at : at + 8], 0, parity_ref[0], picked)
+
     row = pl.program_id(0) * picked + lax.broadcasted_iota(jnp.int32, (picked, tokens), 0)
     chosen = code_ref[0:1, :] == row
     for choice in range(1, TOP):
         chosen = chosen | (code_ref[choice : choice + 1, :] == row)
     onehot = jnp.where(chosen, 1.0, 0.0).astype(jnp.bfloat16)
-    out_ref[0] = dot(onehot, rows_ref[...]).astype(jnp.bfloat16)
-
-
-def shared_kernel(code_ref, prob_ref, rows_ref, gate_up_ref, down_ref, out_ref, mix_ref):
-    parts = gate_up_ref.shape[0]
-    gate_weight = jnp.concatenate([gate_up_ref[p, 0] for p in range(parts)], axis=0)
-    up_weight = jnp.concatenate([gate_up_ref[p, 1] for p in range(parts)], axis=0)
+    out_ref[0] = dot(onehot, normed_ref[...]).astype(jnp.bfloat16)
+
+
+def shared_kernel(parity_ref, info_ref, rows_ref, weight_ref, out_ref, mix_ref):
+    parts, units, _ = weight_ref.shape
+    units = units // 3
+    gate_weight, up_weight, down_weight = [
+        jnp.concatenate([weight_ref[p, at * units : (at + 1) * units] for p in range(parts)], axis=0)
+        for at in range(3)
+    ]
     rows = rows_ref[...]
     act = silu_times(dot_rows(rows, gate_weight), dot_rows(rows, up_weight))
-    out_ref[...] = dot(act, down_ref[...])
+    out_ref[...] = dot(act, down_weight)
+    info = info_ref[...].astype(jnp.float32)
     column = lax.broadcasted_iota(jnp.int32, mix_ref.shape, 1)
     mix = jnp.zeros(mix_ref.shape, jnp.float32)
     for choice in range(TOP):
-        one = slice(choice, choice + 1)
-        mix = jnp.where(code_ref[:, one] == column, prob_ref[:, one], mix)
+        code = row_codes(lambda at: info[:, at : at + 1], choice, parity_ref[0], mix_ref.shape[1] // PLANE)
+        mix = jnp.where(code == column, info[:, 16 + choice : 17 + choice], mix)
     mix_ref[...] = mix.astype(jnp.bfloat16)
 
 
@@ -263,21 +278,25 @@
     out_ref[...] = (dot(mix_ref[...], rows_ref[...]) + shared_ref[...]).astype(jnp.bfloat16)
 
 
-def final_kernel(mixed_ref, parts_ref, out_ref):
-    total = mixed_ref[...]
-    for z in range(parts_ref.shape[0]):
-        total = total + parts_ref[z].astype(jnp.float32)
-    out_ref[...] = total.astype(jnp.bfloat16)
-
-
-def reorder_kernel(table_ref, from_ref, to_ref, sems):
-    copies = []
+def final_kernel(z_ref, mixed_ref, parts_ref, out_ref):
+    tokens = out_ref.shape[0]
+    columns = mixed_ref.shape[2]
+    own = pl.ds(pl.multiple_of(z_ref[0] * tokens, tokens), tokens)
+    for block in range(mixed_ref.shape[0]):
+        at = slice(block * columns, (block + 1) * columns)
+        total = mixed_ref[block, own, :].astype(jnp.float32)
+        for z in range(parts_ref.shape[0]):
+            total = total + parts_ref[z, :, at].astype(jnp.float32)
+        out_ref[:, at] = total.astype(jnp.bfloat16)
+
+
+def reorder_kernel(me_ref, table_ref, from_ref, to_ref):
+    me = me_ref[0]
     for block in range(to_ref.shape[0]):
-        copy = pltpu.make_async_copy(from_ref.at[table_ref[block]], to_ref.at[block], sems.at[block])
-        copy.start()
-        copies.append(copy)
-    for copy in copies:
-        copy.wait()
+        source = table_ref[block]
+        z_steps = (me // PLANE - source // PLANE + Z_SIZE) % Z_SIZE
+        steps = (me % PLANE - source % PLANE + PLANE) % PLANE
+        to_ref[block] = from_ref[z_steps * PLANE + steps]
 
 
 def params(mib):
@@ -288,7 +307,7 @@
     return pl.CostEstimate(flops=int(flops), bytes_accessed=int(moved), transcendentals=0)
 
 
-def route_codes(route_ids, z_index):
+def route_info(route_ids, route_logits, z_index):
     tokens = route_ids.shape[0]
     experts = jnp.arange(EXPERTS, dtype=jnp.int32)
     named = route_ids[:, :, None] == experts[None, None, :]
@@ -297,12 +316,13 @@
     before = (order[None, :] < order[:, None]).astype(jnp.float32)
     ahead = dot(before, member)
     rank = jnp.sum(jnp.where(named, ahead[:, None, :], 0.0), axis=2).astype(jnp.int32)
-    half_experts = EXPERTS // 2
-    per_device = half_experts // PLANE
-    plane_at = (route_ids % half_experts) // per_device
-    in_device = (route_ids % per_device) * Z_SIZE + z_index
-    code = (plane_at * per_device * Z_SIZE + in_device) * CAP + rank
-    return code + (route_ids // half_experts) * (PLANE * per_device * Z_SIZE * CAP)
+    per_device = EXPERTS // 2 // PLANE
+    where_to = route_ids // per_device
+    inside = ((route_ids % per_device) * Z_SIZE + z_index) * CAP + rank
+    probs = jax.nn.softmax(route_logits, axis=-1)
+    pad = ((0, 0), (0, 8 - TOP))
+    columns = [jnp.pad(c.astype(jnp.bfloat16), pad) for c in (where_to, inside, probs)]
+    return jnp.concatenate(columns + [jnp.zeros((tokens, 104), jnp.bfloat16)], axis=1)
 
 
 def shards(
@@ -325,129 +345,147 @@
     tokens, width = residual.shape
     devices = lax.axis_size("seq")
     me = lax.axis_index("seq")
-    z_index = me // PLANE
+    z_index, plane_index = me // PLANE, me % PLANE
     z_groups = [[p + PLANE * z for z in range(Z_SIZE)] for p in range(PLANE)]
     planes = [[p + PLANE * z for p in range(PLANE)] for z in range(Z_SIZE)]
-    same_core = [[core + 2 * chip for chip in range(devices // 2)] for core in range(2)]
-    partner = [(i, i ^ 1) for i in range(devices)]
     bf16, f32 = jnp.bfloat16, jnp.float32
     shape = jax.ShapeDtypeStruct
-
-    turned_weight = lax.all_gather(
-        out_weight.T, "seq", axis=0, tiled=True, axis_index_groups=same_core
-    )
+    scalar = lambda value: jnp.reshape(value, (1,)).astype(jnp.int32)
+    all_tokens = Z_SIZE * tokens
+    part = width // Z_SIZE
+
+    def exchange(array, groups):
+        return lax.all_to_all(
+            array, "seq", split_axis=0, concat_axis=0, tiled=True, axis_index_groups=groups
+        )
 
     own_kv = jnp.concatenate([key_vectors, value_vectors], axis=1)
     behind = [from_behind(own_kv, "seq", offset) for offset in range(REACH, 0, -1)]
 
+    turned_weight = lax.all_gather(
+        out_weight.T, "seq", axis=0, tiled=True, axis_index_groups=planes
+    )
+    own_shared = jnp.concatenate(
+        [jnp.transpose(shared_gate_up, (1, 2, 0)).reshape(-1, width), shared_down], axis=0
+    )
+    shared_weight = lax.all_gather(own_shared, "seq", axis=0, axis_index_groups=planes)
+
+    info = route_info(route_ids, route_logits, z_index)
+    sent_width = width + part + info.shape[1]
+    sent = pl.pallas_call(
+        attention_kernel,
+        out_shape=shape((Z_SIZE, tokens, sent_width), bf16),
+        in_specs=[SMEM, SMEM] + [VMEM] * 8,
+        out_specs=VMEM,
+        compiler_params=params(24),
+        cost_estimate=cost(4 * tokens * 5 * tokens * width, 3 * MIB),
+        name="attention",
+    )(scalar(me * tokens), lengths, queries, *behind, own_kv, residual, info)
+
+    sent, cache_blocks = lax.optimization_barrier((sent, cache_blocks))
     _, block_tokens, layers, kv_heads, head_size = cache_blocks.shape
     per_device = block_tokens // devices
-    outgoing_cache = cache_blocks.reshape(devices, per_device * layers, kv_heads, head_size)
-    handed = lax.all_to_all(outgoing_cache, "seq", split_axis=0, concat_axis=0, tiled=True)
-    cache_out = pl.pallas_call(
-        reorder_kernel,
-        out_shape=shape(handed.shape, bf16),
-        in_specs=[SMEM, ANY],
-        out_specs=ANY,
-        scratch_shapes=[pltpu.SemaphoreType.DMA((devices,))],
-        cost_estimate=cost(0, 2 * handed.size * 2),
-        name="reorder",
-    )(block_table, handed)
-    cache_out = cache_out.reshape(devices, per_device, layers, kv_heads, head_size)
-
-    code = route_codes(route_ids, z_index).astype(f32)
-    probs = jax.nn.softmax(route_logits, axis=-1)
-    pad = ((0, 0), (0, 2))
-    packed = jnp.concatenate([jnp.pad(code, pad), jnp.pad(probs, pad)], axis=1).T
-    packed = lax.all_gather(packed, "seq", axis=0, axis_index_groups=z_groups)
-    gathered_codes = packed[:, :8].astype(jnp.int32) - (z_index % 2) * (PLANE * 4 * Z_SIZE * CAP)
-    all_tokens = Z_SIZE * tokens
-    code_rows = jnp.transpose(gathered_codes, (1, 0, 2)).reshape(8, all_tokens)
-    code_columns = jnp.transpose(gathered_codes, (0, 2, 1)).reshape(all_tokens, 8)
-    prob_columns = jnp.transpose(packed[:, 8:], (0, 2, 1)).reshape(all_tokens, 8)
-
-    shared_both = lax.all_gather(
-        jnp.transpose(shared_gate_up, (1, 2, 0)), "seq", axis=0, axis_index_groups=planes
-    )
-    shared_back = lax.all_gather(
-        shared_down, "seq", axis=0, tiled=True, axis_index_groups=planes
-    )
-
-    first_token = jnp.reshape(me * tokens, (1,)).astype(jnp.int32)
-    heads = pl.pallas_call(
-        attention_kernel,
-        out_shape=shape((tokens, width), bf16),
-        in_specs=[SMEM, SMEM] + [VMEM] * 6,
-        out_specs=VMEM,
+    cache_view = cache_blocks.reshape(Z_SIZE, PLANE, per_device * layers, kv_heads, head_size)
+    in_plane = []
+    for step in range(PLANE):
+        piece = lax.dynamic_index_in_dim(
+            cache_view, (plane_index + step) % PLANE, axis=1, keepdims=False
+        )
+        if step:
+            pairs = [
+                (z * PLANE + p, z * PLANE + (p + step) % PLANE)
+                for z in range(Z_SIZE)
+                for p in range(PLANE)
+            ]
+            piece = lax.ppermute(piece, "seq", pairs)
+        in_plane.append(piece)
+
+    gathered = exchange(sent, z_groups).reshape(all_tokens, sent_width)
+    mixed_part = pl.pallas_call(
+        project_kernel,
+        grid=(1,),
+        out_shape=shape((Z_SIZE, all_tokens, part), bf16),
+        in_specs=[
+            pl.BlockSpec((all_tokens, width), lambda i: (0, 0)),
+            pl.BlockSpec((all_tokens, part), lambda i: (0, width // part)),
+            pl.BlockSpec((part, width), lambda i: (0, 0)),
+        ],
+        out_specs=pl.BlockSpec((Z_SIZE, all_tokens, part), lambda i: (0, 0, 0)),
         compiler_params=params(24),
-        cost_estimate=cost(4 * tokens * 5 * tokens * width, 2 * MIB),
-        name="attention",
-    )(first_token, lengths, queries, *behind, own_kv)
-
-    other_heads = lax.ppermute(heads, "seq", partner)
-    core = jnp.reshape(me % 2, (1,)).astype(jnp.int32)
-    steps = 4
-    half_columns = turned_weight.shape[0]
-    own_out, other_out = pl.pallas_call(
-        lambda *refs: project_kernel(*refs, chunk=out_weight.shape[1]),
-        grid=(steps,),
-        out_shape=[shape((tokens, width), f32)] * 2,
-        in_specs=[
-            SMEM,
-            pl.BlockSpec((tokens, width), lambda i: (0, 0)),
-            pl.BlockSpec((tokens, width), lambda i: (0, 0)),
-            pl.BlockSpec((half_columns // steps, width), lambda i: (i, 0)),
-        ],
-        out_specs=[pl.BlockSpec((tokens, width // steps), lambda i: (0, i))] * 2,
-        compiler_params=params(24),
-        cost_estimate=cost(4 * tokens * width * half_columns, 3 * MIB),
+        cost_estimate=cost(2 * all_tokens * width * part, 3 * MIB),
         name="project",
-    )(core, heads, other_heads, turned_weight)
-    received_out = lax.ppermute(other_out, "seq", partner)
-
-    mixed, normed = pl.pallas_call(
-        norm_kernel,
-        out_shape=[shape((tokens, width), f32), shape((Z_SIZE, tokens, width), bf16)],
-        in_specs=[VMEM] * 4,
-        out_specs=[VMEM] * 2,
-        compiler_params=params(16),
-        cost_estimate=cost(8 * tokens * width, 2 * MIB),
-        name="norm",
-    )(residual, own_out, received_out, norm_gain.reshape(1, width))
-
-    rows = lax.all_to_all(
-        normed, "seq", split_axis=0, concat_axis=0, tiled=True, axis_index_groups=z_groups
-    ).reshape(all_tokens, width)
+    )(gathered, gathered, turned_weight)
+    mixed = exchange(mixed_part, z_groups)
 
     local_halves, _, _, half_ff = expert_gate_up.shape
     per_half = Z_SIZE * CAP
     picked = local_halves * per_half
-    outgoing = pl.pallas_call(
+    info_at = sent_width // 128 - 1
+    parity = scalar(z_index % 2)
+    normed, outgoing = pl.pallas_call(
         pick_kernel,
         grid=(PLANE,),
-        out_shape=shape((PLANE, picked, width), bf16),
+        out_shape=[shape((all_tokens, width), bf16), shape((PLANE, picked, width), bf16)],
         in_specs=[
-            pl.BlockSpec((8, all_tokens), lambda i: (0, 0)),
+            SMEM,
+            pl.BlockSpec((Z_SIZE, all_tokens, part), lambda i: (0, 0, 0)),
+            pl.BlockSpec((1, width), lambda i: (0, 0)),
+            pl.BlockSpec((all_tokens, 128), lambda i: (0, info_at)),
+        ],
+        out_specs=[
             pl.BlockSpec((all_tokens, width), lambda i: (0, 0)),
-        ],
-        out_specs=pl.BlockSpec((1, picked, width), lambda i: (i, 0, 0)),
+            pl.BlockSpec((1, picked, width), lambda i: (i, 0, 0)),
+        ],
+        scratch_shapes=[pltpu.VMEM((8, all_tokens), jnp.int32)],
+        compiler_params=params(24),
+        cost_estimate=cost(2 * PLANE * picked * all_tokens * width, 4 * MIB),
+        name="pick",
+    )(parity, mixed, norm_gain.reshape(1, width), gathered)
+
+    outgoing, in_plane = lax.optimization_barrier((outgoing, in_plane))
+    stacked = jnp.stack(in_plane)
+    arrived_cache = []
+    for step in range(Z_SIZE):
+        piece = lax.dynamic_index_in_dim(stacked, (z_index + step) % Z_SIZE, axis=1, keepdims=False)
+        if step:
+            pairs = [
+                (z * PLANE + p, (z + step) % Z_SIZE * PLANE + p)
+                for z in range(Z_SIZE)
+                for p in range(PLANE)
+            ]
+            piece = lax.ppermute(piece, "seq", pairs)
+        arrived_cache.append(piece)
+    arrived_cache = jnp.concatenate(arrived_cache)
+    cache_out = pl.pallas_call(
+        reorder_kernel,
+        out_shape=shape(arrived_cache.shape, bf16),
+        in_specs=[SMEM, SMEM, VMEM],
+        out_specs=VMEM,
         compiler_params=params(16),
-        cost_estimate=cost(2 * PLANE * picked * all_tokens * width, 3 * MIB),
-        name="pick",
-    )(code_rows, rows)
-
-    arrived = lax.all_to_all(
-        outgoing, "seq", split_axis=0, concat_axis=0, tiled=True, axis_index_groups=planes
-    )
+        cost_estimate=cost(0, 2 * arrived_cache.size * 2),
+        name="reorder",
+    )(scalar(me), block_table, arrived_cache)
+    cache_out = cache_out.reshape(devices, per_device, layers, kv_heads, head_size)
+
+    arrived = exchange(outgoing, planes)
     shared_part, mix = pl.pallas_call(
         shared_kernel,
+        grid=(1,),
         out_shape=[shape((all_tokens, width), f32), shape((all_tokens, PLANE * picked), bf16)],
-        in_specs=[VMEM] * 5,
-        out_specs=[VMEM] * 2,
+        in_specs=[
+            SMEM,
+            pl.BlockSpec((all_tokens, 128), lambda i: (0, info_at)),
+            pl.BlockSpec((all_tokens, width), lambda i: (0, 0)),
+            pl.BlockSpec(shared_weight.shape, lambda i: (0, 0, 0)),
+        ],
+        out_specs=[
+            pl.BlockSpec((all_tokens, width), lambda i: (0, 0)),
+            pl.BlockSpec((all_tokens, PLANE * picked), lambda i: (0, 0)),
+        ],
         compiler_params=params(32),
         cost_estimate=cost(6 * all_tokens * 256 * width, 5 * MIB),
         name="shared_expert",
-    )(code_columns, prob_columns, rows, shared_both, shared_back)
+    )(parity, gathered, normed, shared_weight)
 
     gate_up = jnp.transpose(expert_gate_up, (0, 2, 1, 3))
     returning = pl.pallas_call(
@@ -464,9 +502,7 @@
         cost_estimate=cost(6 * PLANE * picked * half_ff * width, 14 * MIB),
         name="experts",
     )(arrived, gate_up, expert_down)
-    returned = lax.all_to_all(
-        returning, "seq", split_axis=0, concat_axis=0, tiled=True, axis_index_groups=planes
-    ).reshape(PLANE * picked, width)
+    returned = exchange(returning, planes).reshape(PLANE * picked, width)
 
     column_steps = 2
     part_width = width // column_steps
@@ -484,23 +520,16 @@
         cost_estimate=cost(2 * all_tokens * PLANE * picked * width, 5 * MIB),
         name="combine",
     )(mix, returned, shared_part)
-    parts = lax.all_to_all(
-        parts.reshape(Z_SIZE, tokens, width),
-        "seq",
-        split_axis=0,
-        concat_axis=0,
-        tiled=True,
-        axis_index_groups=z_groups,
-    )
+    parts = exchange(parts.reshape(Z_SIZE, tokens, width), z_groups)
     layer_out = pl.pallas_call(
         final_kernel,
         out_shape=shape((tokens, width), bf16),
-        in_specs=[VMEM] * 2,
+        in_specs=[SMEM] + [VMEM] * 2,
         out_specs=VMEM,
         compiler_params=params(16),
-        cost_estimate=cost(5 * tokens * width, MIB),
+        cost_estimate=cost(5 * tokens * width, 2 * MIB),
         name="final",
-    )(mixed, parts)
+    )(scalar(z_index), mixed, parts)
     return (layer_out, cache_out)
 
 

time: 270 us -> 232 us (0.86)
  Pallas kernels: 48.9 us -> 16.2 us
  waiting for transfers between devices: 106 us -> 78.3 us
  local copies, waits for them, and re-layouts: 21 us -> 40.8 us
  blocking collectives: 40.4 us -> 29.1 us
  starting transfers between devices: 35.6 us -> 44.9 us
  other arithmetic: 0.44 us -> 6.44 us
    all_gather x1, waiting for transfers between devices: 43.7 us -> 0.01 us  [shards(): lax.all_gather(out_weight.T, 'seq', axis=0, tiled=True, axis_index_groups...]
    all_gather x2 -> x0, blocking collectives: 40.4 us -> none  [the longest x1 24.3 us: shards(): packed = lax.all_gather(packed, 'seq', axis=0, axis_index_groups=z_groups)]
    pallas_call x6 -> x5, Pallas kernels: 42.2 us -> 9.54 us  [the longest x1 2.78 us: shards(): pl.pallas_call(pick_kernel, grid=(PLANE,), out_shape=[shape((all_tokens,...]
    ppermute x2 -> x10, waiting for transfers between devices: 2.94 us -> 32.6 us  [shards(): piece = lax.ppermute(piece, 'seq', pairs)]
    all_to_all x0 -> x1, blocking collectives: none -> 29.1 us  [exchange(): lax.all_to_all(array, 'seq', split_axis=0, concat_axis=0, tiled=True, axi...]
    unnamed x34 -> x64, local copies, waits for them, and re-layouts: 20 us -> 36.2 us
    ppermute x2 -> x10, starting transfers between devices: 0.14 us -> 12.3 us  [shards(): piece = lax.ppermute(piece, 'seq', pairs)]
    all_to_all x5 -> x4, waiting for transfers between devices: 53.6 us -> 45.6 us  [exchange(): lax.all_to_all(array, 'seq', split_axis=0, concat_axis=0, tiled=True, axi...]
  transfers between devices with their start and end apart: 13 -> 20, of which waited for: 8 -> 6; matrix products, arithmetic and copies ran while one was open for 3% -> 12% of each run, Pallas kernels for 15% -> 5%
where the time goes in v2:
time: 232 us; the launch traced here: 230 us
  waiting for transfers between devices  78.3 us (34%)
  starting transfers between devices  44.9 us (19%)
  local copies, waits for them, and re-layouts  40.8 us (18%)
  blocking collectives  29.1 us (13%)
  Pallas kernels  16.2 us (7%)
  between operations  14.3 us (6%)
  other arithmetic  6.44 us (3%)
    all_to_all x4, waiting for transfers between devices, exchange(): lax.all_to_all(array, 'seq', split_axis=0, concat_axis=0, tiled=True, axi...  45.6 us
    unnamed x64, local copies, waits for them, and re-layouts  36.2 us
    ppermute x10, waiting for transfers between devices, shards(): piece = lax.ppermute(piece, 'seq', pairs)  32.6 us
    all_to_all x1, blocking collectives, exchange(): lax.all_to_all(array, 'seq', split_axis=0, concat_axis=0, tiled=True, axi...  29.1 us
    all_to_all x4, starting transfers between devices, exchange(): lax.all_to_all(array, 'seq', split_axis=0, concat_axis=0, tiled=True, axi...  20.6 us
    ppermute x10, starting transfers between devices, shards(): piece = lax.ppermute(piece, 'seq', pairs)  12.3 us
    ppermute x4, starting transfers between devices, from_behind(): return lax.ppermute(shard, axis, pairs)  12 us
  transfers between devices with their start and end apart: 20, of which 6 were waited for; matrix products, arithmetic and copies ran while one was open for 12% of the time, Pallas kernels for 5%

profile of v2, /device:TPU:10, one launch (start us, length us, event | category | flops | bytes accessed | tf_op | source)
XLA Modules:
  0.0 230.3 jit_solution(12639885487728930265)
XLA Ops:
  8.9 3.4 %collective-permute-start = (bf16[64,1024]{1,0:T(8,128)(2,1)S(1)}, bf16[64,1024]{1,0:T(8,128)(2,1)S(1)}, u32[]{:S(2)}, u32[]{:S(2)}) collective-permute-start(bf16[64,1024]{1,0:T(8,128)(2,1)S(1)} %constant_dynamic-update-slice_fusion.own_ref), channel_id=1, source_target_pairs={{0,4},{1,5},{2,6},{3,7},{4,8},{5,9},{6,10},{7,11},{8,12},{9,13},{1... | collective-permute-start | bytes 393224 | tf_op jit(solution)/shard_map/ppermute | solution.py:28
  12.3 2.6 %collective-permute-start.1 = (bf16[64,1024]{1,0:T(8,128)(2,1)S(1)}, bf16[64,1024]{1,0:T(8,128)(2,1)S(1)}, u32[]{:S(2)}, u32[]{:S(2)}) collective-permute-start(bf16[64,1024]{1,0:T(8,128)(2,1)S(1)} %constant_dynamic-update-slice_fusion.own_ref), channel_id=1, source_target_pairs={{0,3},{1,4},{2,5},{3,6},{4,7},{5,8},{6,9},{7,10},{8,11},{9,12},{10... | collective-permute-start | bytes 393224 | tf_op jit(solution)/shard_map/ppermute | solution.py:28
  14.9 3.4 %collective-permute-start.2 = (bf16[64,1024]{1,0:T(8,128)(2,1)S(1)}, bf16[64,1024]{1,0:T(8,128)(2,1)S(1)}, u32[]{:S(2)}, u32[]{:S(2)}) collective-permute-start(bf16[64,1024]{1,0:T(8,128)(2,1)S(1)} %constant_dynamic-update-slice_fusion.own_ref), channel_id=1, source_target_pairs={{0,2},{1,3},{2,4},{3,5},{4,6},{5,7},{6,8},{7,9},{8,10},{9,11},{10,... | collective-permute-start | bytes 393224 | tf_op jit(solution)/shard_map/ppermute | solution.py:28
  18.3 2.6 %collective-permute-start.3 = (bf16[64,1024]{1,0:T(8,128)(2,1)S(1)}, bf16[64,1024]{1,0:T(8,128)(2,1)S(1)}, u32[]{:S(2)}, u32[]{:S(2)}) collective-permute-start(bf16[64,1024]{1,0:T(8,128)(2,1)S(1)} %constant_dynamic-update-slice_fusion.own_ref), channel_id=1, source_target_pairs={{0,1},{1,2},{2,3},{3,4},{4,5},{5,6},{6,7},{7,8},{8,9},{9,10},{10,1... | collective-permute-start | bytes 393224 | tf_op jit(solution)/shard_map/ppermute | solution.py:28
  28.7 1.9 attention.1
  30.6 29.1 %all_to_all.25 = bf16[4,64,2048]{2,1,0:T(8,128)(2,1)S(1)} all-to-all(bf16[4,64,2048]{2,1,0:T(8,128)(2,1)S(1)} %attention.1), channel_id=1, replica_groups={{0,8,16,24},{1,9,17,25},{2,10,18,26},{3,11,19,27},{4,12,20,28},{5,13,21..., dimensions={0} | all-to-all | bytes 2097152 | tf_op jit(solution)/shard_map/all_to_all | solution.py:358
  62.5 5.4 %all-to-all-start.1 = ((bf16[4,256,384]{2,1,0:T(8,128)(2,1)}), bf16[4,256,384]{2,1,0:T(8,128)(2,1)S(1)}, u32[]{:S(2)}, u32[]{:S(2)}) async-start(bf16[4,256,384]{2,1,0:T(8,128)(2,1)} %project.1), calls=%async_computation.1 | async-start | bytes 1572864 | tf_op jit(solution)/shard_map/all_to_all | solution.py:358
  77.0 7.9 %all-to-all-done.1.mixed_ref = bf16[4,256,384]{2,1,0:T(8,128)(2,1)S(1)} async-done(((bf16[4,256,384]{2,1,0:T(8,128)(2,1)}), bf16[4,256,384]{2,1,0:T(8,128)(2,1)S(1)}, u32[]{:S(2)}, u32[]{:S(2)}) %all-to-all-start.1) | async-done | bytes 786464 | tf_op jit(solution)/shard_map/all_to_all | solution.py:358
  84.9 2.8 %pick.1 = (bf16[256,1536]{1,0:T(8,128)(2,1)S(1)}, bf16[8,96,1536]{2,1,0:T(8,128)(2,1)S(1)}) custom-call(s32[1]{0:T(128)} %bitcast.4.parity_ref, bf16[4,256,384]{2,1,0:T(8,128)(2,1)S(1)} %all-to-all-done.1.mixed_ref, f32[1,1536]{1,0:T(1,128)S(1)} %reshape.45.gain_ref, bf16[256,2048]{1,0:T(8,128)(2,1)S(1)} %bitcast.61), custom_call_target="tpu_custom_call" | custom-call | flops 603979776 | bytes 4194304 | tf_op jit(solution)/shard_map/pick/pallas_call | solution.py:425
  90.8 3.7 %all-to-all-start.2 = ((bf16[8,96,1536]{2,1,0:T(8,128)(2,1)}), bf16[8,96,1536]{2,1,0:T(8,128)(2,1)S(1)}, u32[]{:S(2)}, u32[]{:S(2)}) async-start(bf16[8,96,1536]{2,1,0:T(8,128)(2,1)} %copy-done.5), calls=%async_computation.2 | async-start | bytes 4718592 | tf_op jit(solution)/shard_map/all_to_all | solution.py:358
  96.2 6.3 %copy.42 = bf16[4,1536,2,256]{3,1,2,0:T(8,128)(2,1)} copy(bf16[4,1536,2,256]{3,2,1,0:T(2,128)(2,1)} %param.26) | data formatting | bytes 12582912 | tf_op args[11]
  102.5 23.1 %all-to-all-done.2.rows_ref = bf16[8,96,1536]{2,1,0:T(8,128)(2,1)S(1)} async-done(((bf16[8,96,1536]{2,1,0:T(8,128)(2,1)}), bf16[8,96,1536]{2,1,0:T(8,128)(2,1)S(1)}, u32[]{:S(2)}, u32[]{:S(2)}) %all-to-all-start.2) | async-done | bytes 2359328 | tf_op jit(solution)/shard_map/all_to_all | solution.py:358
  125.6 3.0 %copy-done = bf16[4,1536,2,256]{3,1,2,0:T(8,128)(2,1)S(1)} copy-done((bf16[4,1536,2,256]{3,1,2,0:T(8,128)(2,1)S(1)}, bf16[4,1536,2,256]{3,1,2,0:T(8,128)(2,1)}, u32[]{:S(2)}) %copy-start) | copy-done | bytes 6291480
  128.6 1.9 copy-done.1
  130.5 3.9 %experts.1 = bf16[8,96,1536]{2,1,0:T(8,128)(2,1)} custom-call(bf16[8,96,1536]{2,1,0:T(8,128)(2,1)S(1)} %all-to-all-done.2.rows_ref, bf16[4,2,1536,256]{3,2,1,0:T(8,128)(2,1)S(1)} %bitcast.58, bf16[4,256,1536]{2,1,0:T(8,128)(2,1)S(1)} %copy-done.1), custom_call_target="tpu_custom_call" | custom-call | flops 1811939328 | bytes 14680064 | tf_op jit(solution)/shard_map/experts/pallas_call | solution.py:491
  134.4 5.2 %all-to-all-start.3 = ((bf16[8,96,1536]{2,1,0:T(8,128)(2,1)}), bf16[8,96,1536]{2,1,0:T(8,128)(2,1)S(1)}, u32[]{:S(2)}, u32[]{:S(2)}) async-start(bf16[8,96,1536]{2,1,0:T(8,128)(2,1)} %experts.1), calls=%async_computation.3 | async-start | bytes 4718592 | tf_op jit(solution)/shard_map/all_to_all | solution.py:358
  152.9 14.6 %all-to-all-done.3 = bf16[8,96,1536]{2,1,0:T(8,128)(2,1)S(1)} async-done(((bf16[8,96,1536]{2,1,0:T(8,128)(2,1)}), bf16[8,96,1536]{2,1,0:T(8,128)(2,1)S(1)}, u32[]{:S(2)}, u32[]{:S(2)}) %all-to-all-start.3) | async-done | bytes 2359328 | tf_op jit(solution)/shard_map/all_to_all | solution.py:358
  169.9 2.0 combine.1
  171.9 6.4 %all-to-all-start.4 = ((bf16[4,64,1536]{2,1,0:T(8,128)(2,1)}), bf16[4,64,1536]{2,1,0:T(8,128)(2,1)S(1)}, u32[]{:S(2)}, u32[]{:S(2)}) async-start(bf16[4,64,1536]{2,1,0:T(8,128)(2,1)} %bitcast.19), calls=%async_computation.4 | async-start | bytes 1572864 | tf_op jit(solution)/shard_map/all_to_all | solution.py:358
  185.4 1.9 collective-permute-start.13
  187.4 26.0 %collective-permute-done.11 = bf16[8,32,4,128]{3,2,1,0:T(4,128)(2,1)S(1)} collective-permute-done((bf16[8,32,4,128]{3,2,1,0:T(4,128)(2,1)S(1)}, bf16[8,32,4,128]{3,2,1,0:T(4,128)(2,1)S(1)}, u32[]{:S(2)}, u32[]{:S(2)}) %collective-permute-start.11) | collective-permute-done | bytes 262176 | tf_op jit(solution)/shard_map/ppermute | solution.py:456
  213.3 4.7 %collective-permute-done.12 = bf16[8,32,4,128]{3,2,1,0:T(4,128)(2,1)S(1)} collective-permute-done((bf16[8,32,4,128]{3,2,1,0:T(4,128)(2,1)S(1)}, bf16[8,32,4,128]{3,2,1,0:T(4,128)(2,1)S(1)}, u32[]{:S(2)}, u32[]{:S(2)}) %collective-permute-start.12) | collective-permute-done | bytes 262176 | tf_op jit(solution)/shard_map/ppermute | solution.py:456
  218.1 1.9 collective-permute-done.13
  220.8 1.9 reorder.1
  (111 shorter events, 50.4 us)
Async XLA Ops:
  7.2 52.5 %all-gather.4.cloned.1.call-start = ((), (), s32[]{:S(2)}) async-start(), calls=%async_computation.5 | async-start | bytes 1327104 | tf_op jit(solution)/shard_map/all_gather | solution.py:365
  8.9 17.3 %collective-permute-start = (bf16[64,1024]{1,0:T(8,128)(2,1)S(1)}, bf16[64,1024]{1,0:T(8,128)(2,1)S(1)}, u32[]{:S(2)}, u32[]{:S(2)}) collective-permute-start(bf16[64,1024]{1,0:T(8,128)(2,1)S(1)} %constant_dynamic-update-slice_fusion.own_ref), channel_id=1, source_target_pairs={{0,4},{1,5},{2,6},{3,7},{4,8},{5,9},{6,10},{7,11},{8,12},{9,13},{1... | collective-permute-start | bytes 393224 | tf_op jit(solution)/shard_map/ppermute | solution.py:28
  12.3 13.8 %collective-permute-start.1 = (bf16[64,1024]{1,0:T(8,128)(2,1)S(1)}, bf16[64,1024]{1,0:T(8,128)(2,1)S(1)}, u32[]{:S(2)}, u32[]{:S(2)}) collective-permute-start(bf16[64,1024]{1,0:T(8,128)(2,1)S(1)} %constant_dynamic-update-slice_fusion.own_ref), channel_id=1, source_target_pairs={{0,3},{1,4},{2,5},{3,6},{4,7},{5,8},{6,9},{7,10},{8,11},{9,12},{10... | collective-permute-start | bytes 393224 | tf_op jit(solution)/shard_map/ppermute | solution.py:28
  14.9 11.3 %collective-permute-start.2 = (bf16[64,1024]{1,0:T(8,128)(2,1)S(1)}, bf16[64,1024]{1,0:T(8,128)(2,1)S(1)}, u32[]{:S(2)}, u32[]{:S(2)}) collective-permute-start(bf16[64,1024]{1,0:T(8,128)(2,1)S(1)} %constant_dynamic-update-slice_fusion.own_ref), channel_id=1, source_target_pairs={{0,2},{1,3},{2,4},{3,5},{4,6},{5,7},{6,8},{7,9},{8,10},{9,11},{10,... | collective-permute-start | bytes 393224 | tf_op jit(solution)/shard_map/ppermute | solution.py:28
  18.3 7.9 %collective-permute-start.3 = (bf16[64,1024]{1,0:T(8,128)(2,1)S(1)}, bf16[64,1024]{1,0:T(8,128)(2,1)S(1)}, u32[]{:S(2)}, u32[]{:S(2)}) collective-permute-start(bf16[64,1024]{1,0:T(8,128)(2,1)S(1)} %constant_dynamic-update-slice_fusion.own_ref), channel_id=1, source_target_pairs={{0,1},{1,2},{2,3},{3,4},{4,5},{5,6},{6,7},{7,8},{8,9},{9,10},{10,1... | collective-permute-start | bytes 393224 | tf_op jit(solution)/shard_map/ppermute | solution.py:28
  62.5 14.5 %copy-start.26 = (f32[1536]{0:T(1024)S(1)}, f32[1536]{0:T(1024)}, u32[]{:S(2)}) copy-start(f32[1536]{0:T(1024)} %param.21) | copy-start | bytes 18436
  62.5 22.5 %all-to-all-start.1 = ((bf16[4,256,384]{2,1,0:T(8,128)(2,1)}), bf16[4,256,384]{2,1,0:T(8,128)(2,1)S(1)}, u32[]{:S(2)}, u32[]{:S(2)}) async-start(bf16[4,256,384]{2,1,0:T(8,128)(2,1)} %project.1), calls=%async_computation.1 | async-start | bytes 1572864 | tf_op jit(solution)/shard_map/all_to_all | solution.py:358
  69.1 5.0 %collective-permute-start.10 = (bf16[4,32,4,128]{3,2,1,0:T(4,128)(2,1)S(1)}, bf16[4,32,4,128]{3,2,1,0:T(4,128)(2,1)S(1)}, u32[]{:S(2)}, u32[]{:S(2)}) collective-permute-start(bf16[4,32,4,128]{3,2,1,0:T(4,128)(2,1)S(1)} %get-tuple-element.36), channel_id=1, source_target_pairs={{0,7},{1,0},{2,1},{3,2},{4,3},{5,4},{6,5},{7,6},{8,15},{9,8},{10,9... | collective-permute-start | bytes 393224 | tf_op jit(solution)/shard_map/ppermute | solution.py:400
  69.1 6.7 %collective-permute-start.4 = (bf16[4,32,4,128]{3,2,1,0:T(4,128)(2,1)S(1)}, bf16[4,32,4,128]{3,2,1,0:T(4,128)(2,1)S(1)}, u32[]{:S(2)}, u32[]{:S(2)}) collective-permute-start(bf16[4,32,4,128]{3,2,1,0:T(4,128)(2,1)S(1)} %get-tuple-element.42), channel_id=1, source_target_pairs={{0,1},{1,2},{2,3},{3,4},{4,5},{5,6},{6,7},{7,0},{8,9},{9,10},{10,1... | collective-permute-start | bytes 393224 | tf_op jit(solution)/shard_map/ppermute | solution.py:400
  69.6 20.4 %collective-permute-start.5 = (bf16[4,32,4,128]{3,2,1,0:T(4,128)(2,1)}, bf16[4,32,4,128]{3,2,1,0:T(4,128)(2,1)S(1)}, u32[]{:S(2)}, u32[]{:S(2)}) collective-permute-start(bf16[4,32,4,128]{3,2,1,0:T(4,128)(2,1)} %get-tuple-element.41), channel_id=1, source_target_pairs={{0,2},{1,3},{2,4},{3,5},{4,6},{5,7},{6,0},{7,1},{8,10},{9,11},{10,... | collective-permute-start | bytes 393224 | tf_op jit(solution)/shard_map/ppermute | solution.py:400
  71.2 18.9 %collective-permute-start.6 = (bf16[4,32,4,128]{3,2,1,0:T(4,128)(2,1)S(1)}, bf16[4,32,4,128]{3,2,1,0:T(4,128)(2,1)S(1)}, u32[]{:S(2)}, u32[]{:S(2)}) collective-permute-start(bf16[4,32,4,128]{3,2,1,0:T(4,128)(2,1)S(1)} %get-tuple-element.40), channel_id=1, source_target_pairs={{0,3},{1,4},{2,5},{3,6},{4,7},{5,0},{6,1},{7,2},{8,11},{9,12},{10,... | collective-permute-start | bytes 393224 | tf_op jit(solution)/shard_map/ppermute | solution.py:400
  73.0 17.1 %collective-permute-start.7 = (bf16[4,32,4,128]{3,2,1,0:T(4,128)(2,1)S(1)}, bf16[4,32,4,128]{3,2,1,0:T(4,128)(2,1)S(1)}, u32[]{:S(2)}, u32[]{:S(2)}) collective-permute-start(bf16[4,32,4,128]{3,2,1,0:T(4,128)(2,1)S(1)} %get-tuple-element.39), channel_id=1, source_target_pairs={{0,4},{1,5},{2,6},{3,7},{4,0},{5,1},{6,2},{7,3},{8,12},{9,13},{10,... | collective-permute-start | bytes 393224 | tf_op jit(solution)/shard_map/ppermute | solution.py:400
  74.1 16.0 %collective-permute-start.8 = (bf16[4,32,4,128]{3,2,1,0:T(4,128)(2,1)S(1)}, bf16[4,32,4,128]{3,2,1,0:T(4,128)(2,1)S(1)}, u32[]{:S(2)}, u32[]{:S(2)}) collective-permute-start(bf16[4,32,4,128]{3,2,1,0:T(4,128)(2,1)S(1)} %get-tuple-element.38), channel_id=1, source_target_pairs={{0,5},{1,6},{2,7},{3,0},{4,1},{5,2},{6,3},{7,4},{8,13},{9,14},{10,... | collective-permute-start | bytes 393224 | tf_op jit(solution)/shard_map/ppermute | solution.py:400
  75.8 14.3 %copy-start.22 = (bf16[4,32,4,128]{3,2,1,0:T(4,128)(2,1)}, bf16[4,32,4,128]{3,2,1,0:T(4,128)(2,1)S(1)}, u32[]{:S(2)}) copy-start(bf16[4,32,4,128]{3,2,1,0:T(4,128)(2,1)S(1)} %collective-permute-done.4) | copy-start | bytes 393220
  75.8 14.3 %collective-permute-start.9 = (bf16[4,32,4,128]{3,2,1,0:T(4,128)(2,1)S(1)}, bf16[4,32,4,128]{3,2,1,0:T(4,128)(2,1)}, u32[]{:S(2)}, u32[]{:S(2)}) collective-permute-start(bf16[4,32,4,128]{3,2,1,0:T(4,128)(2,1)S(1)} %get-tuple-element.37), channel_id=1, source_target_pairs={{0,6},{1,7},{2,0},{3,1},{4,2},{5,3},{6,4},{7,5},{8,14},{9,15},{10,... | collective-permute-start | bytes 393224 | tf_op jit(solution)/shard_map/ppermute | solution.py:400
  90.8 34.8 %all-to-all-start.2 = ((bf16[8,96,1536]{2,1,0:T(8,128)(2,1)}), bf16[8,96,1536]{2,1,0:T(8,128)(2,1)S(1)}, u32[]{:S(2)}, u32[]{:S(2)}) async-start(bf16[8,96,1536]{2,1,0:T(8,128)(2,1)} %copy-done.5), calls=%async_computation.2 | async-start | bytes 4718592 | tf_op jit(solution)/shard_map/all_to_all | solution.py:358
  94.5 52.2 %all-gather.6.cloned.1.call-start = ((), (), s32[]{:S(2)}) async-start(), calls=%async_computation.6 | async-start | bytes 2654208 | tf_op jit(solution)/shard_map/all_gather | solution.py:371
  134.4 33.1 %all-to-all-start.3 = ((bf16[8,96,1536]{2,1,0:T(8,128)(2,1)}), bf16[8,96,1536]{2,1,0:T(8,128)(2,1)S(1)}, u32[]{:S(2)}, u32[]{:S(2)}) async-start(bf16[8,96,1536]{2,1,0:T(8,128)(2,1)} %experts.1), calls=%async_computation.3 | async-start | bytes 4718592 | tf_op jit(solution)/shard_map/all_to_all | solution.py:358
  171.9 50.7 %all-to-all-start.4 = ((bf16[4,64,1536]{2,1,0:T(8,128)(2,1)}), bf16[4,64,1536]{2,1,0:T(8,128)(2,1)S(1)}, u32[]{:S(2)}, u32[]{:S(2)}) async-start(bf16[4,64,1536]{2,1,0:T(8,128)(2,1)} %bitcast.19), calls=%async_computation.4 | async-start | bytes 1572864 | tf_op jit(solution)/shard_map/all_to_all | solution.py:358
  179.0 41.7 %copy-start.16 = (s32[32]{0:T(128)S(1)}, s32[32]{0:T(128)}, u32[]{:S(2)}) copy-start(s32[32]{0:T(128)} %table_ref.1) | copy-start | bytes 388
  182.9 39.8 %copy-start.3 = (bf16[4,256,384]{2,1,0:T(8,128)(2,1)S(1)}, bf16[4,256,384]{2,1,0:T(8,128)(2,1)}, u32[]{:S(2)}) copy-start(bf16[4,256,384]{2,1,0:T(8,128)(2,1)} %copy-done.2) | copy-start | bytes 2359300
  182.9 30.4 %collective-permute-start.11 = (bf16[8,32,4,128]{3,2,1,0:T(4,128)(2,1)S(1)}, bf16[8,32,4,128]{3,2,1,0:T(4,128)(2,1)S(1)}, u32[]{:S(2)}, u32[]{:S(2)}) collective-permute-start(bf16[8,32,4,128]{3,2,1,0:T(4,128)(2,1)S(1)} %get-tuple-element.35), channel_id=1, source_target_pairs={{0,8},{1,9},{2,10},{3,11},{4,12},{5,13},{6,14},{7,15},{8,16},{9,17... | collective-permute-start | bytes 786440 | tf_op jit(solution)/shard_map/ppermute | solution.py:456
  184.5 33.6 %collective-permute-start.12 = (bf16[8,32,4,128]{3,2,1,0:T(4,128)(2,1)S(1)}, bf16[8,32,4,128]{3,2,1,0:T(4,128)(2,1)S(1)}, u32[]{:S(2)}, u32[]{:S(2)}) collective-permute-start(bf16[8,32,4,128]{3,2,1,0:T(4,128)(2,1)S(1)} %get-tuple-element.34), channel_id=1, source_target_pairs={{0,16},{1,17},{2,18},{3,19},{4,20},{5,21},{6,22},{7,23},{8,24},{9,... | collective-permute-start | bytes 786440 | tf_op jit(solution)/shard_map/ppermute | solution.py:456
  185.4 34.6 %collective-permute-start.13 = (bf16[8,32,4,128]{3,2,1,0:T(4,128)(2,1)S(1)}, bf16[8,32,4,128]{3,2,1,0:T(4,128)(2,1)S(1)}, u32[]{:S(2)}, u32[]{:S(2)}) collective-permute-start(bf16[8,32,4,128]{3,2,1,0:T(4,128)(2,1)S(1)} %get-tuple-element.33), channel_id=1, source_target_pairs={{0,24},{1,25},{2,26},{3,27},{4,28},{5,29},{6,30},{7,31},{8,0},{9,1... | collective-permute-start | bytes 786440 | tf_op jit(solution)/shard_map/ppermute | solution.py:456
  (23 other events, 55.1 us)
Sparse Core Ops, SparseCore 0:
  21.1 24.0 all-gather.3
  97.2 40.3 all-gather.5

commit v3 on v2

--- a/solution.py
+++ b/solution.py
@@ -204,6 +204,46 @@
                 out_ref[z, :, h * HD : (h + 1) * HD] = result[member * tokens : (member + 1) * tokens]
 
 
+def route_kernel(z_ref, ids_ref, logits_ref, out_ref, turned_ref):
+    choices, tokens = ids_ref.shape
+    turned_ref[...] = jnp.zeros(turned_ref.shape, jnp.float32)
+    turned_ref[:choices, :tokens] = ids_ref[...].astype(jnp.float32)
+    turned_ref[8 : 8 + choices, :tokens] = logits_ref[...]
+    table = turned_ref[...].T[:tokens]
+    lane = lax.broadcasted_iota(jnp.int32, table.shape, 1)
+    ids = [table[:, c : c + 1].astype(jnp.int32) for c in range(choices)]
+    logits = [table[:, 8 + c : 9 + c] for c in range(choices)]
+    member = jnp.zeros(table.shape, jnp.float32)
+    for one in ids:
+        member = jnp.where(lane == one, 1.0, member)
+    row = lax.broadcasted_iota(jnp.int32, (tokens, tokens), 0)
+    earlier = jnp.where(lax.broadcasted_iota(jnp.int32, (tokens, tokens), 1) < row, 1.0, 0.0)
+    ahead = dot(earlier.astype(jnp.bfloat16), member.astype(jnp.bfloat16))
+    top = logits[0]
+    for one in logits[1:]:
+        top = jnp.maximum(top, one)
+    powers = [jnp.exp(one - top) for one in logits]
+    total = sum(powers[1:], powers[0])
+    per_device = EXPERTS // 2 // PLANE
+    out = jnp.zeros(table.shape, jnp.float32)
+    for c, one in enumerate(ids):
+        rank = jnp.sum(jnp.where(lane == one, ahead, 0.0), axis=1, keepdims=True)
+        where_to = lax.div(one, per_device).astype(jnp.float32)
+        first = (lax.rem(one, per_device) * Z_SIZE + z_ref[0]) * CAP
+        out = jnp.where(lane == c, where_to, out)
+        out = jnp.where(lane == 8 + c, first.astype(jnp.float32) + rank, out)
+        out = jnp.where(lane == 16 + c, powers[c] / total, out)
+    out_ref[...] = out.astype(jnp.bfloat16)
+
+
+def regroup_kernel(z_ref, *refs):
+    pieces, outs = refs[:PLANE], refs[PLANE:]
+    for step, out in enumerate(outs):
+        z = lax.rem(z_ref[0] + step, Z_SIZE)
+        for at, piece in enumerate(pieces):
+            out[at] = piece[z]
+
+
 def project_kernel(heads_ref, residual_ref, weight_ref, out_ref):
     out = dot_rows(heads_ref[...], weight_ref[...]) + residual_ref[...].astype(jnp.float32)
     out = out.astype(jnp.bfloat16)
@@ -294,35 +334,17 @@
     me = me_ref[0]
     for block in range(to_ref.shape[0]):
         source = table_ref[block]
-        z_steps = (me // PLANE - source // PLANE + Z_SIZE) % Z_SIZE
-        steps = (me % PLANE - source % PLANE + PLANE) % PLANE
+        z_steps = lax.rem(lax.div(me, PLANE) - lax.div(source, PLANE) + Z_SIZE, Z_SIZE)
+        steps = lax.rem(lax.rem(me, PLANE) - lax.rem(source, PLANE) + PLANE, PLANE)
         to_ref[block] = from_ref[z_steps * PLANE + steps]
 
 
-def params(mib):
-    return pltpu.CompilerParams(vmem_limit_bytes=mib * MIB)
+def params():
+    return pltpu.CompilerParams(vmem_limit_bytes=58 * MIB)
 
 
 def cost(flops, moved):
     return pl.CostEstimate(flops=int(flops), bytes_accessed=int(moved), transcendentals=0)
-
-
-def route_info(route_ids, route_logits, z_index):
-    tokens = route_ids.shape[0]
-    experts = jnp.arange(EXPERTS, dtype=jnp.int32)
-    named = route_ids[:, :, None] == experts[None, None, :]
-    member = jnp.any(named, axis=1).astype(jnp.float32)
-    order = jnp.arange(tokens, dtype=jnp.int32)
-    before = (order[None, :] < order[:, None]).astype(jnp.float32)
-    ahead = dot(before, member)
-    rank = jnp.sum(jnp.where(named, ahead[:, None, :], 0.0), axis=2).astype(jnp.int32)
-    per_device = EXPERTS // 2 // PLANE
-    where_to = route_ids // per_device
-    inside = ((route_ids % per_device) * Z_SIZE + z_index) * CAP + rank
-    probs = jax.nn.softmax(route_logits, axis=-1)
-    pad = ((0, 0), (0, 8 - TOP))
-    columns = [jnp.pad(c.astype(jnp.bfloat16), pad) for c in (where_to, inside, probs)]
-    return jnp.concatenate(columns + [jnp.zeros((tokens, 104), jnp.bfloat16)], axis=1)
 
 
 def shards(
@@ -345,7 +367,7 @@
     tokens, width = residual.shape
     devices = lax.axis_size("seq")
     me = lax.axis_index("seq")
-    z_index, plane_index = me // PLANE, me % PLANE
+    z_index, plane_index = lax.div(me, PLANE), lax.rem(me, PLANE)
     z_groups = [[p + PLANE * z for z in range(Z_SIZE)] for p in range(PLANE)]
     planes = [[p + PLANE * z for p in range(PLANE)] for z in range(Z_SIZE)]
     bf16, f32 = jnp.bfloat16, jnp.float32
@@ -368,28 +390,39 @@
     own_shared = jnp.concatenate(
         [jnp.transpose(shared_gate_up, (1, 2, 0)).reshape(-1, width), shared_down], axis=0
     )
-    shared_weight = lax.all_gather(own_shared, "seq", axis=0, axis_index_groups=planes)
-
-    info = route_info(route_ids, route_logits, z_index)
+
+    info = pl.pallas_call(
+        route_kernel,
+        out_shape=shape((tokens, 128), bf16),
+        in_specs=[SMEM] + [VMEM] * 2,
+        out_specs=VMEM,
+        scratch_shapes=[pltpu.VMEM((128, 128), f32)],
+        compiler_params=params(),
+        cost_estimate=cost(MIB, MIB),
+        name="route",
+    )(scalar(z_index), route_ids.T, route_logits.T)
     sent_width = width + part + info.shape[1]
     sent = pl.pallas_call(
         attention_kernel,
         out_shape=shape((Z_SIZE, tokens, sent_width), bf16),
         in_specs=[SMEM, SMEM] + [VMEM] * 8,
         out_specs=VMEM,
-        compiler_params=params(24),
+        compiler_params=params(),
         cost_estimate=cost(4 * tokens * 5 * tokens * width, 3 * MIB),
         name="attention",
     )(scalar(me * tokens), lengths, queries, *behind, own_kv, residual, info)
 
-    sent, cache_blocks = lax.optimization_barrier((sent, cache_blocks))
+    sent, cache_blocks, own_shared, expert_gate_up = lax.optimization_barrier(
+        (sent, cache_blocks, own_shared, expert_gate_up)
+    )
+    shared_weight = lax.all_gather(own_shared, "seq", axis=0, axis_index_groups=planes)
     _, block_tokens, layers, kv_heads, head_size = cache_blocks.shape
     per_device = block_tokens // devices
     cache_view = cache_blocks.reshape(Z_SIZE, PLANE, per_device * layers, kv_heads, head_size)
     in_plane = []
     for step in range(PLANE):
         piece = lax.dynamic_index_in_dim(
-            cache_view, (plane_index + step) % PLANE, axis=1, keepdims=False
+            cache_view, lax.rem(plane_index + step, PLANE), axis=1, keepdims=False
         )
         if step:
             pairs = [
@@ -411,17 +444,18 @@
             pl.BlockSpec((part, width), lambda i: (0, 0)),
         ],
         out_specs=pl.BlockSpec((Z_SIZE, all_tokens, part), lambda i: (0, 0, 0)),
-        compiler_params=params(24),
+        compiler_params=params(),
         cost_estimate=cost(2 * all_tokens * width * part, 3 * MIB),
         name="project",
     )(gathered, gathered, turned_weight)
+    gate_up = jnp.transpose(expert_gate_up, (0, 2, 1, 3))
     mixed = exchange(mixed_part, z_groups)
 
     local_halves, _, _, half_ff = expert_gate_up.shape
     per_half = Z_SIZE * CAP
     picked = local_halves * per_half
     info_at = sent_width // 128 - 1
-    parity = scalar(z_index % 2)
+    parity = scalar(lax.rem(z_index, 2))
     normed, outgoing = pl.pallas_call(
         pick_kernel,
         grid=(PLANE,),
@@ -437,16 +471,24 @@
             pl.BlockSpec((1, picked, width), lambda i: (i, 0, 0)),
         ],
         scratch_shapes=[pltpu.VMEM((8, all_tokens), jnp.int32)],
-        compiler_params=params(24),
+        compiler_params=params(),
         cost_estimate=cost(2 * PLANE * picked * all_tokens * width, 4 * MIB),
         name="pick",
     )(parity, mixed, norm_gain.reshape(1, width), gathered)
 
-    outgoing, in_plane = lax.optimization_barrier((outgoing, in_plane))
-    stacked = jnp.stack(in_plane)
+    outgoing, in_plane, gate_up = lax.optimization_barrier((outgoing, in_plane, gate_up))
+    along_z = pl.pallas_call(
+        regroup_kernel,
+        out_shape=[shape((PLANE,) + in_plane[0].shape[1:], bf16)] * Z_SIZE,
+        in_specs=[SMEM] + [VMEM] * PLANE,
+        out_specs=[VMEM] * Z_SIZE,
+        compiler_params=params(),
+        cost_estimate=cost(0, 2 * MIB),
+        name="regroup",
+    )(scalar(z_index), *in_plane)
     arrived_cache = []
     for step in range(Z_SIZE):
-        piece = lax.dynamic_index_in_dim(stacked, (z_index + step) % Z_SIZE, axis=1, keepdims=False)
+        piece = along_z[step]
         if step:
             pairs = [
                 (z * PLANE + p, (z + step) % Z_SIZE * PLANE + p)
@@ -455,19 +497,34 @@
             ]
             piece = lax.ppermute(piece, "seq", pairs)
         arrived_cache.append(piece)
+    arrived = exchange(outgoing, planes)
+    returning = pl.pallas_call(
+        experts_kernel,
+        grid=(local_halves // 2,),
+        out_shape=shape((PLANE, picked, width), bf16),
+        in_specs=[
+            pl.BlockSpec((PLANE, 2 * per_half, width), lambda i: (0, i, 0)),
+            pl.BlockSpec((2, 2, width, half_ff), lambda i: (i, 0, 0, 0)),
+            pl.BlockSpec((2, half_ff, width), lambda i: (i, 0, 0)),
+        ],
+        out_specs=pl.BlockSpec((PLANE, 2 * per_half, width), lambda i: (0, i, 0)),
+        compiler_params=params(),
+        cost_estimate=cost(6 * PLANE * picked * half_ff * width, 14 * MIB),
+        name="experts",
+    )(arrived, gate_up, expert_down)
+    returning, arrived_cache = lax.optimization_barrier((returning, arrived_cache))
     arrived_cache = jnp.concatenate(arrived_cache)
     cache_out = pl.pallas_call(
         reorder_kernel,
         out_shape=shape(arrived_cache.shape, bf16),
         in_specs=[SMEM, SMEM, VMEM],
         out_specs=VMEM,
-        compiler_params=params(16),
+        compiler_params=params(),
         cost_estimate=cost(0, 2 * arrived_cache.size * 2),
         name="reorder",
     )(scalar(me), block_table, arrived_cache)
     cache_out = cache_out.reshape(devices, per_device, layers, kv_heads, head_size)
 
-    arrived = exchange(outgoing, planes)
     shared_part, mix = pl.pallas_call(
         shared_kernel,
         grid=(1,),
@@ -482,26 +539,11 @@
             pl.BlockSpec((all_tokens, width), lambda i: (0, 0)),
             pl.BlockSpec((all_tokens, PLANE * picked), lambda i: (0, 0)),
         ],
-        compiler_params=params(32),
+        compiler_params=params(),
         cost_estimate=cost(6 * all_tokens * 256 * width, 5 * MIB),
         name="shared_expert",
     )(parity, gathered, normed, shared_weight)
 
-    gate_up = jnp.transpose(expert_gate_up, (0, 2, 1, 3))
-    returning = pl.pallas_call(
-        experts_kernel,
-        grid=(local_halves // 2,),
-        out_shape=shape((PLANE, picked, width), bf16),
-        in_specs=[
-            pl.BlockSpec((PLANE, 2 * per_half, width), lambda i: (0, i, 0)),
-            pl.BlockSpec((2, 2, width, half_ff), lambda i: (i, 0, 0, 0)),
-            pl.BlockSpec((2, half_ff, width), lambda i: (i, 0, 0)),
-        ],
-        out_specs=pl.BlockSpec((PLANE, 2 * per_half, width), lambda i: (0, i, 0)),
-        compiler_params=params(40),
-        cost_estimate=cost(6 * PLANE * picked * half_ff * width, 14 * MIB),
-        name="experts",
-    )(arrived, gate_up, expert_down)
     returned = exchange(returning, planes).reshape(PLANE * picked, width)
 
     column_steps = 2
@@ -516,7 +558,7 @@
             pl.BlockSpec((all_tokens, part_width), lambda i: (0, i)),
         ],
         out_specs=pl.BlockSpec((all_tokens, part_width), lambda i: (0, i)),
-        compiler_params=params(24),
+        compiler_params=params(),
         cost_estimate=cost(2 * all_tokens * PLANE * picked * width, 5 * MIB),
         name="combine",
     )(mix, returned, shared_part)
@@ -526,7 +568,7 @@
         out_shape=shape((tokens, width), bf16),
         in_specs=[SMEM] + [VMEM] * 2,
         out_specs=VMEM,
-        compiler_params=params(16),
+        compiler_params=params(),
         cost_estimate=cost(5 * tokens * width, 2 * MIB),
         name="final",
     )(scalar(z_index), mixed, parts)

time: 232 us -> 213 us (0.918)
  local copies, waits for them, and re-layouts: 40.8 us -> 16.2 us
  Pallas kernels: 16.2 us -> 37.4 us
  waiting for transfers between devices: 78.3 us -> 64 us
  other arithmetic: 6.44 us -> 3.47 us
    ppermute x10, waiting for transfers between devices: 32.6 us -> 3.29 us  [shards(): piece = lax.ppermute(piece, 'seq', pairs)]
    unnamed x64 -> x39, local copies, waits for them, and re-layouts: 36.2 us -> 7.09 us
    all_to_all x4, waiting for transfers between devices: 45.6 us -> 59.3 us  [exchange(): lax.all_to_all(array, 'seq', split_axis=0, concat_axis=0, tiled=True, axi...]
    optimization_barrier x0 -> x1, local copies, waits for them, and re-layouts: none -> 6.31 us  [shards(): lax.optimization_barrier((sent, cache_blocks, own_shared, expert_gate_up))]
    pallas_call x0 -> x2, Pallas kernels: none -> 4.9 us  [the longest x1 2.56 us: shards(): pl.pallas_call(route_kernel, out_shape=shape((tokens, 128), bf16), in_spe...]
    pallas_call x1, Pallas kernels: 2.78 us -> 5.91 us  [shards(): pl.pallas_call(pick_kernel, grid=(PLANE,), out_shape=[shape((all_tokens,...]
    pallas_call x1, Pallas kernels: 1.48 us -> 4.58 us  [shards(): pl.pallas_call(shared_kernel, grid=(1,), out_shape=[shape((all_tokens, wi...]
    pallas_call x1, Pallas kernels: 3.87 us -> 6.8 us  [shards(): pl.pallas_call(experts_kernel, grid=(local_halves // 2,), out_shape=shape...]
  transfers between devices with their start and end apart: 20 -> 20, of which waited for: 6 -> 4; matrix products, arithmetic and copies ran while one was open for 12% -> 6% of each run, Pallas kernels for 5% -> 14%
where the time goes in v3:
time: 213 us; the launch traced here: 209 us
  waiting for transfers between devices  64 us (30%)
  starting transfers between devices  45.8 us (22%)
  Pallas kernels  37.4 us (18%)
  blocking collectives  28.2 us (13%)
  local copies, waits for them, and re-layouts  16.2 us (8%)
  between operations  14.2 us (7%)
  other arithmetic  3.47 us (2%)
    all_to_all x4, waiting for transfers between devices, exchange(): lax.all_to_all(array, 'seq', split_axis=0, concat_axis=0, tiled=True, axi...  59.3 us
    all_to_all x1, blocking collectives, exchange(): lax.all_to_all(array, 'seq', split_axis=0, concat_axis=0, tiled=True, axi...  28.2 us
    all_to_all x4, starting transfers between devices, exchange(): lax.all_to_all(array, 'seq', split_axis=0, concat_axis=0, tiled=True, axi...  20.4 us
    ppermute x4, starting transfers between devices, from_behind(): return lax.ppermute(shard, axis, pairs)  13.1 us
    ppermute x10, starting transfers between devices, shards(): piece = lax.ppermute(piece, 'seq', pairs)  12.3 us
    unnamed x39, local copies, waits for them, and re-layouts  7.09 us
    pallas_call x1, Pallas kernels, shards(): pl.pallas_call(experts_kernel, grid=(local_halves // 2,), out_shape=shape...  6.8 us
    optimization_barrier x1, local copies, waits for them, and re-layouts, shards(): lax.optimization_barrier((sent, cache_blocks, own_shared, expert_gate_up))  6.31 us
  transfers between devices with their start and end apart: 20, of which 4 were waited for; matrix products, arithmetic and copies ran while one was open for 6% of the time, Pallas kernels for 14%

profile of v3, /device:TPU:10, one launch (start us, length us, event | category | flops | bytes accessed | tf_op | source)
XLA Modules:
  0.0 209.4 jit_solution(1666260456241777901)
XLA Ops:
  11.5 3.4 %collective-permute-start.2 = (bf16[64,1024]{1,0:T(8,128)(2,1)S(1)}, bf16[64,1024]{1,0:T(8,128)(2,1)S(1)}, u32[]{:S(2)}, u32[]{:S(2)}) collective-permute-start(bf16[64,1024]{1,0:T(8,128)(2,1)S(1)} %constant_dynamic-update-slice_fusion.own_ref), channel_id=1, source_target_pairs={{0,2},{1,3},{2,4},{3,5},{4,6},{5,7},{6,8},{7,9},{8,10},{9,11},{10,... | collective-permute-start | bytes 393224 | tf_op jit(solution)/shard_map/ppermute | solution.py:28
  14.9 4.3 %collective-permute-start.1 = (bf16[64,1024]{1,0:T(8,128)(2,1)S(1)}, bf16[64,1024]{1,0:T(8,128)(2,1)S(1)}, u32[]{:S(2)}, u32[]{:S(2)}) collective-permute-start(bf16[64,1024]{1,0:T(8,128)(2,1)S(1)} %constant_dynamic-update-slice_fusion.own_ref), channel_id=1, source_target_pairs={{0,3},{1,4},{2,5},{3,6},{4,7},{5,8},{6,9},{7,10},{8,11},{9,12},{10... | collective-permute-start | bytes 393224 | tf_op jit(solution)/shard_map/ppermute | solution.py:28
  19.2 3.4 %collective-permute-start = (bf16[64,1024]{1,0:T(8,128)(2,1)S(1)}, bf16[64,1024]{1,0:T(8,128)(2,1)S(1)}, u32[]{:S(2)}, u32[]{:S(2)}) collective-permute-start(bf16[64,1024]{1,0:T(8,128)(2,1)S(1)} %constant_dynamic-update-slice_fusion.own_ref), channel_id=1, source_target_pairs={{0,4},{1,5},{2,6},{3,7},{4,8},{5,9},{6,10},{7,11},{8,12},{9,13},{1... | collective-permute-start | bytes 393224 | tf_op jit(solution)/shard_map/ppermute | solution.py:28
  22.7 2.6 %route.1.info_ref = bf16[64,128]{1,0:T(8,128)(2,1)} custom-call(s32[1]{0:T(128)} %bitcast.z_ref, s32[6,64]{1,0:T(8,128)} %bitcast.63, f32[6,64]{1,0:T(8,128)} %bitcast.64), custom_call_target="tpu_custom_call" | custom-call | flops 1048576 | bytes 1048576 | tf_op jit(solution)/shard_map/route/pallas_call | solution.py:394
  27.7 3.6 %attention.1 = bf16[4,64,2048]{2,1,0:T(8,128)(2,1)} custom-call(s32[1]{0:T(128)} %bitcast.1.first_ref, s32[16]{0:T(128)} %lengths_ref.1, bf16[64,1536]{1,0:T(8,128)(2,1)} %q_ref.1, bf16[64,1024]{1,0:T(8,128)(2,1)} %copy-done.17, bf16[64,1024]{1,0:T(8,128)(2,1)} %copy-done.16, bf16[64,1024]{1,0:T(8,128)(2,1)} %copy-done.15, bf16[64,1024]{1,0:T(8,128)(2,1)} %copy-done.14, ...), custom_call_target="tpu_custom_call" | custom-call | flops 125829120 | bytes 3145728 | tf_op jit(solution)/shard_map/attention/pallas_call | solution.py:405
  31.4 28.2 %all_to_all.25 = bf16[4,64,2048]{2,1,0:T(8,128)(2,1)} all-to-all(bf16[4,64,2048]{2,1,0:T(8,128)(2,1)} %attention.1), channel_id=1, replica_groups={{0,8,16,24},{1,9,17,25},{2,10,18,26},{3,11,19,27},{4,12,20,28},{5,13,21..., dimensions={0} | all-to-all | bytes 2097152 | tf_op jit(solution)/shard_map/all_to_all | solution.py:380
  59.6 3.2 %project.1 = bf16[4,256,384]{2,1,0:T(8,128)(2,1)} custom-call(bf16[256,2048]{1,0:T(8,128)(2,1)} %bitcast.52, bf16[256,2048]{1,0:T(8,128)(2,1)} %bitcast.53, bf16[384,1536]{1,0:T(8,128)(2,1)} %all-gather.4.cloned.1.call-done.weight_ref), custom_call_target="tpu_custom_call" | custom-call | flops 301989888 | bytes 3145728 | tf_op jit(solution)/shard_map/project/pallas_call | solution.py:437
  62.8 5.4 %all-to-all-start.1 = ((bf16[4,256,384]{2,1,0:T(8,128)(2,1)}), bf16[4,256,384]{2,1,0:T(8,128)(2,1)S(1)}, u32[]{:S(2)}, u32[]{:S(2)}) async-start(bf16[4,256,384]{2,1,0:T(8,128)(2,1)} %project.1), calls=%async_computation.1 | async-start | bytes 1572864 | tf_op jit(solution)/shard_map/all_to_all | solution.py:380
  73.4 2.4 %collective-permute-start.6 = (bf16[4,32,4,128]{3,2,1,0:T(4,128)(2,1)S(1)}, bf16[4,32,4,128]{3,2,1,0:T(4,128)(2,1)S(1)}, u32[]{:S(2)}, u32[]{:S(2)}) collective-permute-start(bf16[4,32,4,128]{3,2,1,0:T(4,128)(2,1)S(1)} %get-tuple-element.60), channel_id=1, source_target_pairs={{0,3},{1,4},{2,5},{3,6},{4,7},{5,0},{6,1},{7,2},{8,11},{9,12},{10,... | collective-permute-start | bytes 393224 | tf_op jit(solution)/shard_map/ppermute | solution.py:433
  76.8 3.3 %collective-permute-done.9.refs_6_ = bf16[4,32,4,128]{3,2,1,0:T(4,128)(2,1)S(1)} collective-permute-done((bf16[4,32,4,128]{3,2,1,0:T(4,128)(2,1)S(1)}, bf16[4,32,4,128]{3,2,1,0:T(4,128)(2,1)S(1)}, u32[]{:S(2)}, u32[]{:S(2)}) %collective-permute-start.9) | collective-permute-done | bytes 131104 | tf_op jit(solution)/shard_map/ppermute | solution.py:433
  80.7 6.3 %copy.35 = bf16[4,1536,2,256]{3,1,2,0:T(8,128)(2,1)} copy(bf16[4,1536,2,256]{3,2,1,0:T(2,128)(2,1)} %param.26) | data formatting | bytes 12582912 | tf_op jit(solution)/shard_map/optimization_barrier | solution.py:415
  87.9 5.9 %pick.1 = (bf16[256,1536]{1,0:T(8,128)(2,1)}, bf16[8,96,1536]{2,1,0:T(8,128)(2,1)}) custom-call(s32[1]{0:T(128)} %bitcast.8.parity_ref, bf16[4,256,384]{2,1,0:T(8,128)(2,1)} %copy-done.2, f32[1,1536]{1,0:T(1,128)} %reshape.44.gain_ref, bf16[256,2048]{1,0:T(8,128)(2,1)} %bitcast.54), custom_call_target="tpu_custom_call" | custom-call | flops 603979776 | bytes 4194304 | tf_op jit(solution)/shard_map/pick/pallas_call | solution.py:459
  94.7 3.6 %all-to-all-start.2 = ((bf16[8,96,1536]{2,1,0:T(8,128)(2,1)}), bf16[8,96,1536]{2,1,0:T(8,128)(2,1)S(1)}, u32[]{:S(2)}, u32[]{:S(2)}) async-start(bf16[8,96,1536]{2,1,0:T(8,128)(2,1)} %get-tuple-element.36), calls=%async_computation.2 | async-start | bytes 4718592 | tf_op jit(solution)/shard_map/all_to_all | solution.py:380
  99.0 2.3 %regroup.1 = (bf16[8,32,4,128]{3,2,1,0:T(4,128)(2,1)}, bf16[8,32,4,128]{3,2,1,0:T(4,128)(2,1)}, bf16[8,32,4,128]{3,2,1,0:T(4,128)(2,1)}, bf16[8,32,4,128]{3,2,1,0:T(4,128)(2,1)}) custom-call(s32[1]{0:T(128)} %bitcast.z_ref, bf16[4,32,4,128]{3,2,1,0:T(4,128)(2,1)} %get-tuple-element.38.refs_0_, bf16[4,32,4,128]{3,2,1,0:T(4,128)(2,1)} %copy-done.13, ...), custom_call_target="tpu_custom_call" | custom-call | bytes 2097152 | tf_op jit(solution)/shard_map/regroup/pallas_call | solution.py:480
  102.8 3.5 %collective-permute-start.12 = (bf16[8,32,4,128]{3,2,1,0:T(4,128)(2,1)}, bf16[8,32,4,128]{3,2,1,0:T(4,128)(2,1)S(1)}, u32[]{:S(2)}, u32[]{:S(2)}) collective-permute-start(bf16[8,32,4,128]{3,2,1,0:T(4,128)(2,1)} %get-tuple-element.48), channel_id=1, source_target_pairs={{0,16},{1,17},{2,18},{3,19},{4,20},{5,21},{6,22},{7,23},{8,24},{9,... | collective-permute-start | bytes 786440 | tf_op jit(solution)/shard_map/ppermute | solution.py:498
  106.3 22.8 %all-to-all-done.2.rows_ref = bf16[8,96,1536]{2,1,0:T(8,128)(2,1)S(1)} async-done(((bf16[8,96,1536]{2,1,0:T(8,128)(2,1)}), bf16[8,96,1536]{2,1,0:T(8,128)(2,1)S(1)}, u32[]{:S(2)}, u32[]{:S(2)}) %all-to-all-start.2) | async-done | bytes 2359328 | tf_op jit(solution)/shard_map/all_to_all | solution.py:380
  130.7 6.8 %experts.1 = bf16[8,96,1536]{2,1,0:T(8,128)(2,1)} custom-call(bf16[8,96,1536]{2,1,0:T(8,128)(2,1)} %copy-done, bf16[4,2,1536,256]{3,2,1,0:T(8,128)(2,1)} %bitcast.51, bf16[4,256,1536]{2,1,0:T(8,128)(2,1)} %down_ref.1), custom_call_target="tpu_custom_call" | custom-call | flops 1811939328 | bytes 14680064 | tf_op jit(solution)/shard_map/experts/pallas_call | solution.py:501
  137.5 5.1 %all-to-all-start.3 = ((bf16[8,96,1536]{2,1,0:T(8,128)(2,1)}), bf16[8,96,1536]{2,1,0:T(8,128)(2,1)S(1)}, u32[]{:S(2)}, u32[]{:S(2)}) async-start(bf16[8,96,1536]{2,1,0:T(8,128)(2,1)} %experts.1), calls=%async_computation.3 | async-start | bytes 4718592 | tf_op jit(solution)/shard_map/all_to_all | solution.py:380
  142.5 4.6 %shared_expert.1 = (f32[256,1536]{1,0:T(8,128)}, bf16[256,768]{1,0:T(8,128)(2,1)}) custom-call(s32[1]{0:T(128)} %bitcast.8.parity_ref, bf16[256,2048]{1,0:T(8,128)(2,1)} %bitcast.55, bf16[256,1536]{1,0:T(8,128)(2,1)} %get-tuple-element.30.rows_ref, bf16[8,96,1536]{2,1,0:T(8,128)(2,1)} %bitcast.58), custom_call_target="tpu_custom_call" | custom-call | flops 603979776 | bytes 5242880 | tf_op jit(solution)/shard_map/shared_expert/pallas_call | solution.py:528
  147.1 23.4 %all-to-all-done.3 = bf16[8,96,1536]{2,1,0:T(8,128)(2,1)S(1)} async-done(((bf16[8,96,1536]{2,1,0:T(8,128)(2,1)}), bf16[8,96,1536]{2,1,0:T(8,128)(2,1)S(1)}, u32[]{:S(2)}, u32[]{:S(2)}) %all-to-all-start.3) | async-done | bytes 2359328 | tf_op jit(solution)/shard_map/all_to_all | solution.py:380
  171.9 3.8 %combine.1 = bf16[256,1536]{1,0:T(8,128)(2,1)} custom-call(bf16[256,768]{1,0:T(8,128)(2,1)} %get-tuple-element.32.mix_ref, bf16[768,1536]{1,0:T(8,128)(2,1)} %bitcast.56, f32[256,1536]{1,0:T(8,128)} %get-tuple-element.51.shared_ref), custom_call_target="tpu_custom_call" | custom-call | flops 603979776 | bytes 5242880 | tf_op jit(solution)/shard_map/combine/pallas_call | solution.py:551
  175.7 6.4 %all-to-all-start.4 = ((bf16[4,64,1536]{2,1,0:T(8,128)(2,1)}), bf16[4,64,1536]{2,1,0:T(8,128)(2,1)S(1)}, u32[]{:S(2)}, u32[]{:S(2)}) async-start(bf16[4,64,1536]{2,1,0:T(8,128)(2,1)} %bitcast.57), calls=%async_computation.4 | async-start | bytes 1572864 | tf_op jit(solution)/shard_map/all_to_all | solution.py:380
  183.9 2.5 %reorder.1 = bf16[32,32,4,128]{3,2,1,0:T(4,128)(2,1)} custom-call(s32[1]{0:T(128)} %bitcast.22.me_ref, s32[32]{0:T(128)} %table_ref.1, bf16[32,32,4,128]{3,2,1,0:T(4,128)(2,1)} %pad_maximum_fusion.from_ref), custom_call_target="tpu_custom_call" | custom-call | bytes 2097152 | tf_op jit(solution)/shard_map/reorder/pallas_call | solution.py:517
  186.3 13.1 %all-to-all-done.4.parts_ref = bf16[4,64,1536]{2,1,0:T(8,128)(2,1)S(1)} async-done(((bf16[4,64,1536]{2,1,0:T(8,128)(2,1)}), bf16[4,64,1536]{2,1,0:T(8,128)(2,1)S(1)}, u32[]{:S(2)}, u32[]{:S(2)}) %all-to-all-start.4) | async-done | bytes 786464 | tf_op jit(solution)/shard_map/all_to_all | solution.py:380
  (74 shorter events, 25.3 us)
Async XLA Ops:
  7.2 52.4 %all-gather.4.cloned.1.call-start = ((), (), s32[]{:S(2)}) async-start(), calls=%async_computation.5 | async-start | bytes 1327104 | tf_op jit(solution)/shard_map/all_gather | solution.py:387
  9.6 17.4 %copy-start.5 = (bf16[64,1024]{1,0:T(8,128)(2,1)}, bf16[64,1024]{1,0:T(8,128)(2,1)S(1)}, u32[]{:S(2)}) copy-start(bf16[64,1024]{1,0:T(8,128)(2,1)S(1)} %constant_dynamic-update-slice_fusion.own_ref) | copy-start | bytes 393220
  9.6 17.4 %collective-permute-start.3 = (bf16[64,1024]{1,0:T(8,128)(2,1)S(1)}, bf16[64,1024]{1,0:T(8,128)(2,1)S(1)}, u32[]{:S(2)}, u32[]{:S(2)}) collective-permute-start(bf16[64,1024]{1,0:T(8,128)(2,1)S(1)} %constant_dynamic-update-slice_fusion.own_ref), channel_id=1, source_target_pairs={{0,1},{1,2},{2,3},{3,4},{4,5},{5,6},{6,7},{7,8},{8,9},{9,10},{10,1... | collective-permute-start | bytes 393224 | tf_op jit(solution)/shard_map/ppermute | solution.py:28
  11.5 15.5 %collective-permute-start.2 = (bf16[64,1024]{1,0:T(8,128)(2,1)S(1)}, bf16[64,1024]{1,0:T(8,128)(2,1)S(1)}, u32[]{:S(2)}, u32[]{:S(2)}) collective-permute-start(bf16[64,1024]{1,0:T(8,128)(2,1)S(1)} %constant_dynamic-update-slice_fusion.own_ref), channel_id=1, source_target_pairs={{0,2},{1,3},{2,4},{3,5},{4,6},{5,7},{6,8},{7,9},{8,10},{9,11},{10,... | collective-permute-start | bytes 393224 | tf_op jit(solution)/shard_map/ppermute | solution.py:28
  14.9 12.1 %collective-permute-start.1 = (bf16[64,1024]{1,0:T(8,128)(2,1)S(1)}, bf16[64,1024]{1,0:T(8,128)(2,1)S(1)}, u32[]{:S(2)}, u32[]{:S(2)}) collective-permute-start(bf16[64,1024]{1,0:T(8,128)(2,1)S(1)} %constant_dynamic-update-slice_fusion.own_ref), channel_id=1, source_target_pairs={{0,3},{1,4},{2,5},{3,6},{4,7},{5,8},{6,9},{7,10},{8,11},{9,12},{10... | collective-permute-start | bytes 393224 | tf_op jit(solution)/shard_map/ppermute | solution.py:28
  19.2 7.8 %collective-permute-start = (bf16[64,1024]{1,0:T(8,128)(2,1)S(1)}, bf16[64,1024]{1,0:T(8,128)(2,1)S(1)}, u32[]{:S(2)}, u32[]{:S(2)}) collective-permute-start(bf16[64,1024]{1,0:T(8,128)(2,1)S(1)} %constant_dynamic-update-slice_fusion.own_ref), channel_id=1, source_target_pairs={{0,4},{1,5},{2,6},{3,7},{4,8},{5,9},{6,10},{7,11},{8,12},{9,13},{1... | collective-permute-start | bytes 393224 | tf_op jit(solution)/shard_map/ppermute | solution.py:28
  62.8 17.3 %copy-start.18 = (f32[1536]{0:T(1024)S(1)}, f32[1536]{0:T(1024)}, u32[]{:S(2)}) copy-start(f32[1536]{0:T(1024)} %param.21) | copy-start | bytes 18436
  62.8 24.2 %all-to-all-start.1 = ((bf16[4,256,384]{2,1,0:T(8,128)(2,1)}), bf16[4,256,384]{2,1,0:T(8,128)(2,1)S(1)}, u32[]{:S(2)}, u32[]{:S(2)}) async-start(bf16[4,256,384]{2,1,0:T(8,128)(2,1)} %project.1), calls=%async_computation.1 | async-start | bytes 1572864 | tf_op jit(solution)/shard_map/all_to_all | solution.py:380
  69.4 6.3 %collective-permute-start.10 = (bf16[4,32,4,128]{3,2,1,0:T(4,128)(2,1)S(1)}, bf16[4,32,4,128]{3,2,1,0:T(4,128)(2,1)S(1)}, u32[]{:S(2)}, u32[]{:S(2)}) collective-permute-start(bf16[4,32,4,128]{3,2,1,0:T(4,128)(2,1)S(1)} %get-tuple-element.56), channel_id=1, source_target_pairs={{0,7},{1,0},{2,1},{3,2},{4,3},{5,4},{6,5},{7,6},{8,15},{9,8},{10,9... | collective-permute-start | bytes 393224 | tf_op jit(solution)/shard_map/ppermute | solution.py:433
  69.5 10.6 %collective-permute-start.9 = (bf16[4,32,4,128]{3,2,1,0:T(4,128)(2,1)S(1)}, bf16[4,32,4,128]{3,2,1,0:T(4,128)(2,1)S(1)}, u32[]{:S(2)}, u32[]{:S(2)}) collective-permute-start(bf16[4,32,4,128]{3,2,1,0:T(4,128)(2,1)S(1)} %get-tuple-element.57), channel_id=1, source_target_pairs={{0,6},{1,7},{2,0},{3,1},{4,2},{5,3},{6,4},{7,5},{8,14},{9,15},{10,... | collective-permute-start | bytes 393224 | tf_op jit(solution)/shard_map/ppermute | solution.py:433
  71.2 22.6 %collective-permute-start.8 = (bf16[4,32,4,128]{3,2,1,0:T(4,128)(2,1)S(1)}, bf16[4,32,4,128]{3,2,1,0:T(4,128)(2,1)S(1)}, u32[]{:S(2)}, u32[]{:S(2)}) collective-permute-start(bf16[4,32,4,128]{3,2,1,0:T(4,128)(2,1)S(1)} %get-tuple-element.58), channel_id=1, source_target_pairs={{0,5},{1,6},{2,7},{3,0},{4,1},{5,2},{6,3},{7,4},{8,13},{9,14},{10,... | collective-permute-start | bytes 393224 | tf_op jit(solution)/shard_map/ppermute | solution.py:433
  73.2 20.6 %collective-permute-start.7 = (bf16[4,32,4,128]{3,2,1,0:T(4,128)(2,1)S(1)}, bf16[4,32,4,128]{3,2,1,0:T(4,128)(2,1)S(1)}, u32[]{:S(2)}, u32[]{:S(2)}) collective-permute-start(bf16[4,32,4,128]{3,2,1,0:T(4,128)(2,1)S(1)} %get-tuple-element.59), channel_id=1, source_target_pairs={{0,4},{1,5},{2,6},{3,7},{4,0},{5,1},{6,2},{7,3},{8,12},{9,13},{10,... | collective-permute-start | bytes 393224 | tf_op jit(solution)/shard_map/ppermute | solution.py:433
  73.4 20.5 %collective-permute-start.6 = (bf16[4,32,4,128]{3,2,1,0:T(4,128)(2,1)S(1)}, bf16[4,32,4,128]{3,2,1,0:T(4,128)(2,1)S(1)}, u32[]{:S(2)}, u32[]{:S(2)}) collective-permute-start(bf16[4,32,4,128]{3,2,1,0:T(4,128)(2,1)S(1)} %get-tuple-element.60), channel_id=1, source_target_pairs={{0,3},{1,4},{2,5},{3,6},{4,7},{5,0},{6,1},{7,2},{8,11},{9,12},{10,... | collective-permute-start | bytes 393224 | tf_op jit(solution)/shard_map/ppermute | solution.py:433
  75.8 11.2 %copy-start.7 = (bf16[4,32,4,128]{3,2,1,0:T(4,128)(2,1)}, bf16[4,32,4,128]{3,2,1,0:T(4,128)(2,1)S(1)}, u32[]{:S(2)}) copy-start(bf16[4,32,4,128]{3,2,1,0:T(4,128)(2,1)S(1)} %collective-permute-done.10.refs_7_) | copy-start | bytes 393220
  75.8 18.1 %collective-permute-start.5 = (bf16[4,32,4,128]{3,2,1,0:T(4,128)(2,1)S(1)}, bf16[4,32,4,128]{3,2,1,0:T(4,128)(2,1)S(1)}, u32[]{:S(2)}, u32[]{:S(2)}) collective-permute-start(bf16[4,32,4,128]{3,2,1,0:T(4,128)(2,1)S(1)} %get-tuple-element.61), channel_id=1, source_target_pairs={{0,2},{1,3},{2,4},{3,5},{4,6},{5,7},{6,0},{7,1},{8,10},{9,11},{10,... | collective-permute-start | bytes 393224 | tf_op jit(solution)/shard_map/ppermute | solution.py:433
  80.0 13.9 %collective-permute-start.4 = (bf16[4,32,4,128]{3,2,1,0:T(4,128)(2,1)S(1)}, bf16[4,32,4,128]{3,2,1,0:T(4,128)(2,1)S(1)}, u32[]{:S(2)}, u32[]{:S(2)}) collective-permute-start(bf16[4,32,4,128]{3,2,1,0:T(4,128)(2,1)S(1)} %get-tuple-element.62), channel_id=1, source_target_pairs={{0,1},{1,2},{2,3},{3,4},{4,5},{5,6},{6,7},{7,0},{8,9},{9,10},{10,1... | collective-permute-start | bytes 393224 | tf_op jit(solution)/shard_map/ppermute | solution.py:433
  94.7 34.5 %all-to-all-start.2 = ((bf16[8,96,1536]{2,1,0:T(8,128)(2,1)}), bf16[8,96,1536]{2,1,0:T(8,128)(2,1)S(1)}, u32[]{:S(2)}, u32[]{:S(2)}) async-start(bf16[8,96,1536]{2,1,0:T(8,128)(2,1)} %get-tuple-element.36), calls=%async_computation.2 | async-start | bytes 4718592 | tf_op jit(solution)/shard_map/all_to_all | solution.py:380
  98.3 44.3 %all-gather.6.cloned.1.call-start = ((), (), s32[]{:S(2)}) async-start(), calls=%async_computation.6 | async-start | bytes 2654208 | tf_op jit(solution)/shard_map/all_gather | solution.py:418
  101.3 36.1 %collective-permute-start.11 = (bf16[8,32,4,128]{3,2,1,0:T(4,128)(2,1)}, bf16[8,32,4,128]{3,2,1,0:T(4,128)(2,1)S(1)}, u32[]{:S(2)}, u32[]{:S(2)}) collective-permute-start(bf16[8,32,4,128]{3,2,1,0:T(4,128)(2,1)} %get-tuple-element.47), channel_id=1, source_target_pairs={{0,8},{1,9},{2,10},{3,11},{4,12},{5,13},{6,14},{7,15},{8,16},{9,17... | collective-permute-start | bytes 786440 | tf_op jit(solution)/shard_map/ppermute | solution.py:498
  102.8 34.6 %collective-permute-start.12 = (bf16[8,32,4,128]{3,2,1,0:T(4,128)(2,1)}, bf16[8,32,4,128]{3,2,1,0:T(4,128)(2,1)S(1)}, u32[]{:S(2)}, u32[]{:S(2)}) collective-permute-start(bf16[8,32,4,128]{3,2,1,0:T(4,128)(2,1)} %get-tuple-element.48), channel_id=1, source_target_pairs={{0,16},{1,17},{2,18},{3,19},{4,20},{5,21},{6,22},{7,23},{8,24},{9,... | collective-permute-start | bytes 786440 | tf_op jit(solution)/shard_map/ppermute | solution.py:498
  106.3 31.1 %collective-permute-start.13 = (bf16[8,32,4,128]{3,2,1,0:T(4,128)(2,1)}, bf16[8,32,4,128]{3,2,1,0:T(4,128)(2,1)S(1)}, u32[]{:S(2)}, u32[]{:S(2)}) collective-permute-start(bf16[8,32,4,128]{3,2,1,0:T(4,128)(2,1)} %get-tuple-element.49), channel_id=1, source_target_pairs={{0,24},{1,25},{2,26},{3,27},{4,28},{5,29},{6,30},{7,31},{8,0},{9,1... | collective-permute-start | bytes 786440 | tf_op jit(solution)/shard_map/ppermute | solution.py:498
  137.5 33.0 %all-to-all-start.3 = ((bf16[8,96,1536]{2,1,0:T(8,128)(2,1)}), bf16[8,96,1536]{2,1,0:T(8,128)(2,1)S(1)}, u32[]{:S(2)}, u32[]{:S(2)}) async-start(bf16[8,96,1536]{2,1,0:T(8,128)(2,1)} %experts.1), calls=%async_computation.3 | async-start | bytes 4718592 | tf_op jit(solution)/shard_map/all_to_all | solution.py:380
  171.9 10.2 %copy-start.6 = (bf16[8,32,4,128]{3,2,1,0:T(4,128)(2,1)S(1)}, bf16[8,32,4,128]{3,2,1,0:T(4,128)(2,1)}, u32[]{:S(2)}) copy-start(bf16[8,32,4,128]{3,2,1,0:T(4,128)(2,1)} %get-tuple-element.52) | copy-start | bytes 786436
  175.7 23.7 %all-to-all-start.4 = ((bf16[4,64,1536]{2,1,0:T(8,128)(2,1)}), bf16[4,64,1536]{2,1,0:T(8,128)(2,1)S(1)}, u32[]{:S(2)}, u32[]{:S(2)}) async-start(bf16[4,64,1536]{2,1,0:T(8,128)(2,1)} %bitcast.57), calls=%async_computation.4 | async-start | bytes 1572864 | tf_op jit(solution)/shard_map/all_to_all | solution.py:380
  (15 other events, 26.8 us)
Sparse Core Ops, SparseCore 0:
  9.9 30.4 all-gather.3
  101.0 39.7 all-gather.5
